TPU v7x, 512 devices: a whole 4x8x8 slice. The times are simulated.
512 devices in a mesh: blk: 64 (over x, y_lo, z), grp: 8 (over y_hi, core).
Axes of the slice: x: 4, y: 8 (y_hi: 4, y_lo: 2; y = y_hi * 2 + y_lo), z: 8, core: 2. Of those that a mesh axis runs over, the one named last changes fastest.
Arguments:
- user_factors: float32 [524288, 256], P(('grp', 'blk')), parts along dimension 0, may hold values from -1.5 to 1.5
- item_factors: float32 [262144, 256], P(('grp', 'blk')), parts along dimension 0, may hold values from -1.5 to 1.5
- ratings: bfloat16 [24576, 128, 128], P(('grp', 'blk')), parts along dimension 0, may hold values from -4.1 to 4.1, as said below
- tile_lists: int32 [2048, 2, 12], P(('grp', 'blk')), parts along dimension 0, may hold values from 0 to 3, as said below
- tile_counts: int32 [2048], P(('grp', 'blk')), parts along dimension 0, may hold values from 2 to 12, as said below
Outputs:
- new_users: float32 [524288, 256], P(('grp', 'blk')), parts along dimension 0
- new_items: float32 [262144, 256], P(('grp', 'blk')), parts along dimension 0
There are 8 independent parts, one for each index of `grp`. A program takes and returns all parts, laid end to end along the dimension named above; each array names one. Nothing has to cross between parts.
Inputs may be any that keep to these rules, and one draw needn't show every extreme that they name: `ratings`: zero marks a missing rating; every other entry lies at least 0.1 away from zero. `tile_lists`: the 12 slots of one list name distinct tile positions; row 0 is below 4 and row 1 below 4; slots at or after the list's count hold arbitrary positions and tiles. `tile_counts`: some list of every draw is full.
All inputs are finite; a program needn't handle non-finite values.
Results may differ from a plain program's by a relative error of at most 0.0003.
Values may be sent and summed in bfloat16 or wider, within the bound.
No kernel may reach another device: no remote copies, remote signals or barrier semaphores. Data moves between devices by JAX's collectives and lax.ppermute only.
A program may use at most 64 MiB of HBM per device.

v0:
```python
import jax
import jax.numpy as jnp
from jax import lax
from jax.sharding import PartitionSpec as P

TILE = 128
BATCHES = 2
VISITS = 2
SLOTS = 12


LEARN = 0.02
DECAY = 0.05


def passed_along(value, axis, steps):
    count = lax.axis_size(axis)
    pairs = [(source, (source + steps) % count) for source in range(count)]
    return lax.ppermute(value, axis, pairs)


def batch_step(user_rows, item_block, tile_block, tile_pairs, live_count):
    width = user_rows.shape[1]
    user_tiles = user_rows.reshape(-1, TILE, width)
    item_tiles = item_block.reshape(-1, TILE, width)

    def slot_step(slot_index, carry):
        grad_users, grad_items = carry
        row_pos = tile_pairs[0, slot_index]
        col_pos = tile_pairs[1, slot_index]
        user_tile = lax.dynamic_index_in_dim(user_tiles, row_pos, 0, keepdims=False)
        item_tile = lax.dynamic_index_in_dim(item_tiles, col_pos, 0, keepdims=False)
        observed = lax.dynamic_index_in_dim(tile_block, slot_index, 0, keepdims=False).astype(
            jnp.float32
        )
        predicted = jnp.dot(
            user_tile,
            item_tile.T,
            precision=lax.Precision.HIGHEST,
            preferred_element_type=jnp.float32,
        )
        residue = jnp.where(observed != 0, predicted - observed, 0.0)
        grad_users = grad_users.at[row_pos].add(
            jnp.dot(
                residue,
                item_tile,
                precision=lax.Precision.HIGHEST,
                preferred_element_type=jnp.float32,
            )
        )
        grad_items = grad_items.at[col_pos].add(
            jnp.dot(
                residue.T,
                user_tile,
                precision=lax.Precision.HIGHEST,
                preferred_element_type=jnp.float32,
            )
        )
        return (grad_users, grad_items)

    grad_users, grad_items = lax.fori_loop(
        0, live_count, slot_step, (jnp.zeros_like(user_tiles), jnp.zeros_like(item_tiles))
    )
    new_rows = user_rows - LEARN * (grad_users.reshape(user_rows.shape) + DECAY * user_rows)
    new_block = item_block - LEARN * (grad_items.reshape(item_block.shape) + DECAY * item_block)
    return (new_rows, new_block)


def one_visit(user_rows, item_block, tile_block, tile_pairs, live_counts):
    batch_rows = user_rows.shape[0] // BATCHES
    pieces = []
    for batch_index in range(BATCHES):
        part = user_rows[batch_index * batch_rows : (batch_index + 1) * batch_rows]
        tiles_now = tile_block[batch_index * SLOTS : (batch_index + 1) * SLOTS]
        part, item_block = batch_step(
            part, item_block, tiles_now, tile_pairs[batch_index], live_counts[batch_index]
        )
        pieces.append(part)
    return (jnp.concatenate(pieces, axis=0), item_block)


def on_device(user_factors, item_factors, ratings, tile_lists, tile_counts):
    per_visit = ratings.shape[0] // VISITS
    first_tiles = ratings[:per_visit]
    later_tiles = ratings[per_visit : 2 * per_visit]
    first_pairs = tile_lists[:BATCHES]
    later_pairs = tile_lists[BATCHES : 2 * BATCHES]
    first_counts = tile_counts[:BATCHES]
    later_counts = tile_counts[BATCHES : 2 * BATCHES]
    user_rows, item_block = one_visit(
        user_factors, item_factors, first_tiles, first_pairs, first_counts
    )
    arrived = passed_along(item_block, "blk", 1)
    user_rows, arrived = one_visit(user_rows, arrived, later_tiles, later_pairs, later_counts)
    item_block = passed_along(arrived, "blk", -1)
    return (user_rows, item_block)


def solution(mesh):
    in_specs = (
        P(("grp", "blk"), None),
        P(("grp", "blk"), None),
        P(("grp", "blk"), None, None),
        P(("grp", "blk"), None, None),
        P(("grp", "blk")),
    )
    out_specs = (P(("grp", "blk"), None), P(("grp", "blk"), None))
    return jax.shard_map(
        on_device, mesh=mesh, in_specs=in_specs, out_specs=out_specs, check_vma=False
    )
```

profile of v0, /device:TPU:79, one launch (start us, length us, event | category | flops | bytes accessed | tf_op | source)
XLA Modules:
  0.0 407.3 jit_solution(5380763295264719465)
XLA Ops:
  0.7 2.5 fusion.88
  4.8 18.2 %while.56 = (s32[]{:T(128)}, f32[4,128,256]{2,1,0:T(8,128)S(1)}, f32[4,128,256]{2,1,0:T(8,128)S(1)}, s32[]{:T(128)}, s32[2,12]{1,0:T(2,128)S(1)}, /*index=5*/bf1...) while((s32[]{:T(128)}, f32[4,128,256]{2,1,0:T(8,128)S(1)}, ...), condition=%wide.region_3.4_spmd, body=%wide.region_0.3_spmd.sunk | while | flops 151191584 | bytes 1278263 | solution.py:61
  10.0 1.0 fusion.141
  18.8 1.0 fusion.141
  23.2 99.5 %while.57 = (s32[]{:T(128)}, f32[4,128,256]{2,1,0:T(8,128)S(1)}, f32[4,128,256]{2,1,0:T(8,128)S(1)}, s32[]{:T(128)}, s32[2,12]{1,0:T(2,128)S(1)}, /*index=5*/bf1...) while((s32[]{:T(128)}, f32[4,128,256]{2,1,0:T(8,128)S(1)}, ...), condition=%wide.region_7.8_spmd, body=%wide.region_4.7_spmd.sunk | while | flops 151191584 | bytes 1278263 | solution.py:61
  30.5 1.0 fusion.151
  38.8 1.0 fusion.151
  63.5 1.0 fusion.151
  71.7 1.0 fusion.151
  80.0 1.0 fusion.151
  104.7 1.0 fusion.151
  112.9 1.0 fusion.151
  123.6 49.9 %collective-permute-start = (f32[512,256]{1,0:T(8,128)}, f32[512,256]{1,0:T(8,128)S(1)}, u32[]{:S(2)}, u32[]{:S(2)}) collective-permute-start(f32[512,256]{1,0:T(8,128)} %fusion.83), channel_id=1, source_target_pairs={{0,8},{8,16},{16,24},{24,32},{32,40},{40,48},{48,56},{56,64},{64,7... | collective-permute-start | bytes 1572872 | tf_op jit(solution)/shard_map/ppermute | solution.py:19
  173.5 1.4 fusion.87
  174.9 5.0 %collective-permute-done = f32[512,256]{1,0:T(8,128)S(1)} collective-permute-done((f32[512,256]{1,0:T(8,128)}, f32[512,256]{1,0:T(8,128)S(1)}, u32[]{:S(2)}, u32[]{:S(2)}) %collective-permute-start) | collective-permute-done | bytes 524320 | tf_op jit(solution)/shard_map/ppermute | solution.py:19
  180.0 100.8 %while.58 = (s32[]{:T(128)}, f32[4,128,256]{2,1,0:T(8,128)S(1)}, f32[4,128,256]{2,1,0:T(8,128)S(1)}, s32[]{:T(128)}, s32[2,12]{1,0:T(2,128)S(1)}, /*index=5*/bf1...) while((s32[]{:T(128)}, f32[4,128,256]{2,1,0:T(8,128)S(1)}, ...), condition=%wide.region_11.12_spmd, body=%wide.region_8.11_spmd.sunk | while | flops 151191584 | bytes 1278263 | solution.py:61
  184.9 1.0 fusion.159
  193.2 1.0 fusion.159
  201.5 1.0 fusion.159
  209.9 1.0 fusion.159
  218.2 1.0 fusion.159
  226.6 1.0 fusion.159
  234.9 1.0 fusion.159
  243.3 1.0 fusion.159
  251.6 1.0 fusion.159
  260.0 1.0 fusion.159
  268.3 1.0 fusion.159
  276.6 1.0 fusion.159
  281.0 40.8 %while.59 = (s32[]{:T(128)}, f32[4,128,256]{2,1,0:T(8,128)S(1)}, f32[4,128,256]{2,1,0:T(8,128)S(1)}, s32[]{:T(128)}, s32[2,12]{1,0:T(2,128)S(1)}, /*index=5*/bf1...) while((s32[]{:T(128)}, f32[4,128,256]{2,1,0:T(8,128)S(1)}, ...), condition=%wide.region_15.16_spmd, body=%wide.region_12.15_spmd.sunk | while | flops 151191584 | bytes 1278263 | solution.py:61
  321.9 1.9 collective-permute-start.1
  324.0 1.0 pad_maximum_fusion
  325.0 81.5 %collective-permute-done.1 = f32[512,256]{1,0:T(8,128)S(1)} collective-permute-done((f32[512,256]{1,0:T(8,128)S(1)}, f32[512,256]{1,0:T(8,128)S(1)}, u32[]{:S(2)}, u32[]{:S(2)}) %collective-permute-start.1) | collective-permute-done | bytes 524320 | tf_op jit(solution)/shard_map/ppermute | solution.py:19
  (161 shorter events, 100.1 us)
Async XLA Ops:
  0.6 2.5 copy-start.4
  0.6 2.5 copy-start.3
  0.7 3.1 copy-start.1
  3.8 1.0 copy-start
  3.8 1.0 copy-start.2
  123.6 56.3 %collective-permute-start = (f32[512,256]{1,0:T(8,128)}, f32[512,256]{1,0:T(8,128)S(1)}, u32[]{:S(2)}, u32[]{:S(2)}) collective-permute-start(f32[512,256]{1,0:T(8,128)} %fusion.83), channel_id=1, source_target_pairs={{0,8},{8,16},{16,24},{24,32},{32,40},{40,48},{48,56},{56,64},{64,7... | collective-permute-start | bytes 1572872 | tf_op jit(solution)/shard_map/ppermute | solution.py:19
  321.9 84.6 %collective-permute-start.1 = (f32[512,256]{1,0:T(8,128)S(1)}, f32[512,256]{1,0:T(8,128)S(1)}, u32[]{:S(2)}, u32[]{:S(2)}) collective-permute-start(f32[512,256]{1,0:T(8,128)S(1)} %fusion.73), channel_id=1, source_target_pairs={{0,504},{8,0},{16,8},{24,16},{32,24},{40,32},{48,40},{56,48},{64,5... | collective-permute-start | bytes 1572872 | tf_op jit(solution)/shard_map/ppermute | solution.py:19
where the time goes:
time: 413 us; the launch traced here: 407 us
  loops' own time  142 us (34%)
  waiting for transfers between devices  86.5 us (21%)
  matrix products  74.5 us (18%)
  starting transfers between devices  51.8 us (13%)
  other arithmetic  27.4 us (7%)
  local copies, waits for them, and re-layouts  24.5 us (6%)
    another operation x4, loops' own time, batch_step(): lax.fori_loop(0, live_count, slot_step, (jnp.zeros_like(user_tiles), jnp....  142 us
    ppermute x2, waiting for transfers between devices, passed_along(): return lax.ppermute(value, axis, pairs)  86.5 us
    ppermute x2, starting transfers between devices, passed_along(): return lax.ppermute(value, axis, pairs)  51.8 us
    dot_general x31, matrix products, slot_step(): jnp.dot(residue, item_tile, precision=lax.Precision.HIGHEST, preferred_el...  27.6 us
    dot_general x31, matrix products, slot_step(): jnp.dot(residue.T, user_tile, precision=lax.Precision.HIGHEST, preferred_...  27.4 us
    another operation x31, other arithmetic  23.6 us
    dot_general x31, matrix products, slot_step(): jnp.dot(user_tile, item_tile.T, precision=lax.Precision.HIGHEST, preferre...  19.5 us
    dynamic_slice x31, local copies, waits for them, and re-layouts, slot_step(): col_pos = tile_pairs[1, slot_index]  19.3 us
  transfers between devices with their start and end apart: 2, of which 2 were waited for; matrix products, arithmetic and copies ran while one was open for 1% of the time, Pallas kernels for 0%

commit v1 on v0

v1 whole, which is shorter than its diff:
```python
import jax
import jax.numpy as jnp
from jax import lax
from jax.experimental import pallas as pl
from jax.experimental.pallas import tpu as pltpu
from jax.sharding import PartitionSpec as P

TILE = 128
BATCHES = 2
VISITS = 2
SLOTS = 12
SIDE = 4
PLACES = SIDE * SIDE
ROWS = SIDE * TILE
RANK = 256
HALVES = 2
HALF = ROWS // HALVES
EXTRA = 16
CODED = HALF + EXTRA
LISTED = BATCHES * SLOTS

LEARN = 0.02
DECAY = 0.05
TOP = 32766.0
F32 = jnp.float32
BF16 = jnp.bfloat16


def passed_along(value, axis, steps):
    count = lax.axis_size(axis)
    pairs = [(source, (source + steps) % count) for source in range(count)]
    return lax.ppermute(value, axis, pairs)


def split(value):
    high = value.astype(BF16)
    low = (value - high.astype(F32)).astype(BF16)
    return high, low


def product(left, right, dims):
    def dot(a, b):
        return lax.dot_general(a, b, (dims, ((), ())), preferred_element_type=F32)

    return dot(left[0], right[0]) + (dot(left[1], right[0]) + dot(left[0], right[1]))


def encode(block):
    peak = jnp.maximum(jnp.max(jnp.abs(block), axis=0, keepdims=True), 1e-30)
    power = jnp.ceil(jnp.log2(peak))
    unit = jnp.exp2(power - 8.0)
    units = jnp.ceil(peak / unit)
    coded = jnp.round(block * (TOP / (units * unit))).astype(jnp.int32)
    row = lax.broadcasted_iota(jnp.int32, (EXTRA, RANK), 0)
    scale = jnp.where(
        row == 0, power.astype(jnp.int32), jnp.where(row == 1, units.astype(jnp.int32), 0)
    )
    return coded.astype(jnp.int16), scale.astype(jnp.int16)


def decode(coded, scale):
    scale = scale.astype(jnp.int32).astype(F32)
    step = scale[1:2] * jnp.exp2(scale[0:1] - 8.0) * (1.0 / TOP)
    return coded.astype(jnp.int32).astype(F32) * step


def visit_kernel(
    visit, lists_in, counts_in, users_in, items_in, ratings_in, users_out, items_out,
    users, items, tiles, lists, counts, where, users_high, users_low, grads, sems,
):
    user_copies, tile_copies, out_copies = [], [], []
    list_copy = pltpu.make_async_copy(lists_in, lists, sems.at[7])
    count_copy = pltpu.make_async_copy(counts_in, counts, sems.at[8])
    list_copy.start()
    count_copy.start()
    if visit == 0:
        item_copy = pltpu.make_async_copy(items_in, items, sems.at[4])
        item_copy.start()
        old_users, new_users = users, users_out
    else:
        old_users, new_users = users_in, users
    for batch in range(BATCHES):
        rows = pl.ds(batch * ROWS, ROWS)
        if visit == 0:
            user_copies.append(
                pltpu.make_async_copy(users_in.at[rows], users.at[rows], sems.at[batch])
            )
            user_copies[-1].start()
        first = visit * LISTED + batch * SLOTS
        tile_copies.append(
            pltpu.make_async_copy(
                ratings_in.at[pl.ds(first, SLOTS)],
                tiles.at[pl.ds(batch * SLOTS, SLOTS)],
                sems.at[2 + batch],
            )
        )
        tile_copies[-1].start()
    tiles[LISTED] = jnp.zeros((TILE, TILE), BF16)
    list_copy.wait()
    count_copy.wait()
    for batch in range(BATCHES):
        entry = visit * BATCHES + batch
        for place in range(PLACES):
            where[batch * PLACES + place] = LISTED

        def note(slot, carry):
            place = lists[entry, 0, slot] * SIDE + lists[entry, 1, slot]
            where[batch * PLACES + place] = batch * SLOTS + slot
            return carry

        lax.fori_loop(0, counts[entry], note, 0)

    def residue(predicted, batch, half):
        highs, lows = [], []
        for user_tile in range(SIDE):
            high_row, low_row = [], []
            for item_tile in range(SIDE // HALVES):
                place = user_tile * SIDE + half * (SIDE // HALVES) + item_tile
                observed = tiles[where[batch * PLACES + place]].astype(F32)
                part = predicted[
                    user_tile * TILE : (user_tile + 1) * TILE,
                    item_tile * TILE : (item_tile + 1) * TILE,
                ]
                high, low = split(jnp.where(observed != 0, part - observed, 0.0))
                high_row.append(high)
                low_row.append(low)
            highs.append(jnp.concatenate(high_row, axis=1))
            lows.append(jnp.concatenate(low_row, axis=1))
        return jnp.concatenate(highs, axis=0), jnp.concatenate(lows, axis=0)

    for half in range(HALVES):
        span = pl.ds(half * HALF, HALF)
        if visit == 0:
            if half == 0:
                item_copy.wait()
            block = items[span]
        else:
            block = decode(items_in[half, :HALF], items_in[half, HALF:])
        for batch in range(BATCHES):
            rows = pl.ds(batch * ROWS, ROWS)
            if half == 0:
                if visit == 0:
                    user_copies[batch].wait()
                high, low = split(old_users[rows])
                users_high[rows] = high
                users_low[rows] = low
            batch_users = (users_high[rows], users_low[rows])
            block_parts = split(block)
            predicted = product(batch_users, block_parts, ((1,), (1,)))
            if half == 0:
                tile_copies[batch].wait()
            left = residue(predicted, batch, half)
            grad_users = product(left, block_parts, ((1,), (0,)))
            if half == 0:
                grads[rows] = grad_users
            else:
                old = old_users[rows]
                new_users[rows] = old - LEARN * ((grads[rows] + grad_users) + DECAY * old)
                if visit == 1:
                    out_copies.append(
                        pltpu.make_async_copy(
                            users.at[rows], users_out.at[rows], sems.at[5 + batch]
                        )
                    )
                    out_copies[-1].start()
            grad_items = product(left, batch_users, ((0,), (0,)))
            block = block - LEARN * (grad_items + DECAY * block)
        coded, scale = encode(block)
        items_out[half, :HALF] = coded
        items_out[half, HALF:] = scale
    for copy in out_copies:
        copy.wait()


def held(value):
    return pltpu.with_memory_space_constraint(value, pltpu.HBM)


def visit_call(visit, lists, counts, users, items, ratings):
    spec_hbm = pl.BlockSpec(memory_space=pltpu.HBM)
    spec_vmem = pl.BlockSpec(memory_space=pltpu.VMEM)

    def kernel(*refs):
        visit_kernel(visit, *refs)

    return pl.pallas_call(
        kernel,
        out_shape=(
            jax.ShapeDtypeStruct((BATCHES * ROWS, RANK), F32),
            jax.ShapeDtypeStruct((HALVES, CODED, RANK), jnp.int16),
        ),
        in_specs=[
            spec_hbm,
            spec_hbm,
            spec_hbm if visit == 0 else spec_vmem,
            spec_hbm if visit == 0 else spec_vmem,
            spec_hbm,
        ],
        out_specs=(spec_vmem if visit == 0 else spec_hbm, spec_vmem),
        scratch_shapes=[
            pltpu.VMEM((BATCHES * ROWS, RANK), F32),
            pltpu.VMEM((ROWS, RANK), F32),
            pltpu.VMEM((LISTED + 1, TILE, TILE), BF16),
            pltpu.SMEM((VISITS * BATCHES, 2, SLOTS), jnp.int32),
            pltpu.SMEM((VISITS * BATCHES,), jnp.int32),
            pltpu.SMEM((BATCHES * PLACES,), jnp.int32),
            pltpu.VMEM((BATCHES * ROWS, RANK), BF16),
            pltpu.VMEM((BATCHES * ROWS, RANK), BF16),
            pltpu.VMEM((BATCHES * ROWS, RANK), F32),
            pltpu.SemaphoreType.DMA((9,)),
        ],
        compiler_params=pltpu.CompilerParams(vmem_limit_bytes=40 * 1024 * 1024),
        name=f"visit{visit}",
    )(
        held(lists),
        held(counts),
        held(users) if visit == 0 else users,
        held(items) if visit == 0 else items,
        held(ratings),
    )


def decode_kernel(coded, items):
    for half in range(HALVES):
        items[half * HALF : (half + 1) * HALF] = decode(coded[half, :HALF], coded[half, HALF:])


def decode_call(coded):
    spec_vmem = pl.BlockSpec(memory_space=pltpu.VMEM)
    return pl.pallas_call(
        decode_kernel,
        out_shape=jax.ShapeDtypeStruct((ROWS, RANK), F32),
        in_specs=[spec_vmem],
        out_specs=spec_vmem,
        compiler_params=pltpu.CompilerParams(vmem_limit_bytes=8 * 1024 * 1024),
        name="unpack",
    )(coded)


def on_device(user_factors, item_factors, ratings, tile_lists, tile_counts):
    users, coded = visit_call(0, tile_lists, tile_counts, user_factors, item_factors, ratings)
    arrived = passed_along(coded, "blk", 1)
    users, coded = visit_call(1, tile_lists, tile_counts, users, arrived, ratings)
    items = decode_call(passed_along(coded, "blk", -1))
    return (users, items)


def solution(mesh):
    in_specs = (
        P(("grp", "blk"), None),
        P(("grp", "blk"), None),
        P(("grp", "blk"), None, None),
        P(("grp", "blk"), None, None),
        P(("grp", "blk")),
    )
    out_specs = (P(("grp", "blk"), None), P(("grp", "blk"), None))
    return jax.shard_map(
        on_device, mesh=mesh, in_specs=in_specs, out_specs=out_specs, check_vma=False
    )
```

time: 413 us -> 44.6 us (0.11)
  the two profiles are of different devices: /device:TPU:79 before, /device:TPU:16 now
where the time goes in v1:
time: 44.6 us; the launch traced here: 44.4 us
  waiting for transfers between devices  22.6 us (51%)
  Pallas kernels  13.1 us (29%)
  starting transfers between devices  8 us (18%)
  between operations  0.66 us (1%)
    ppermute x2, waiting for transfers between devices, passed_along(): return lax.ppermute(value, axis, pairs)  22.6 us
    pallas_call x2, Pallas kernels, visit_call(): pl.pallas_call(kernel, out_shape=(jax.ShapeDtypeStruct((BATCHES * ROWS, R...  12.3 us
    ppermute x2, starting transfers between devices, passed_along(): return lax.ppermute(value, axis, pairs)  8 us
  transfers between devices with their start and end apart: 2, of which 2 were waited for; matrix products, arithmetic and copies ran while one was open for 0% of the time, Pallas kernels for 0%

profile of v1, /device:TPU:16, one launch (start us, length us, event | category | flops | bytes accessed | tf_op | source)
XLA Modules:
  0.0 44.4 jit_solution(232302032357743123)
XLA Ops:
  0.6 6.0 %visit0.1 = (f32[1024,256]{1,0:T(8,128)S(1)}, s16[2,272,256]{2,1,0:T(8,128)(2,1)S(1)}) custom-call(s32[4,2,12]{2,1,0:T(2,128)} %refs_0_.3, s32[4]{0:T(128)} %refs_1_.3, f32[1024,256]{1,0:T(8,128)} %refs_2_.1, f32[512,256]{1,0:T(8,128)} %refs_3_.1, bf16[48,128,128]{2,1,0:T(8,128)(2,1)} %refs_4_.3), custom_call_target="tpu_custom_call" | custom-call | tf_op jit(solution)/shard_map/visit0/pallas_call | solution.py:186
  6.7 4.3 %collective-permute-start = (s16[2,272,256]{2,1,0:T(8,128)(2,1)S(1)}, s16[2,272,256]{2,1,0:T(8,128)(2,1)S(1)}, u32[]{:S(2)}, u32[]{:S(2)}) collective-permute-start(s16[2,272,256]{2,1,0:T(8,128)(2,1)S(1)} %get-tuple-element.7), channel_id=1, source_target_pairs={{0,8},{8,16},{16,24},{24,32},{32,40},{40,48},{48,56},{56,64},{64,7... | collective-permute-start | bytes 835592 | tf_op jit(solution)/shard_map/ppermute | solution.py:32
  11.0 16.5 %collective-permute-done.refs_3_ = s16[2,272,256]{2,1,0:T(8,128)(2,1)S(1)} collective-permute-done((s16[2,272,256]{2,1,0:T(8,128)(2,1)S(1)}, s16[2,272,256]{2,1,0:T(8,128)(2,1)S(1)}, u32[]{:S(2)}, u32[]{:S(2)}) %collective-permute-start) | collective-permute-done | bytes 278560 | tf_op jit(solution)/shard_map/ppermute | solution.py:32
  27.5 6.2 %visit1.1 = (f32[1024,256]{1,0:T(8,128)}, s16[2,272,256]{2,1,0:T(8,128)(2,1)S(1)}) custom-call(s32[4,2,12]{2,1,0:T(2,128)} %refs_0_.3, s32[4]{0:T(128)} %refs_1_.3, f32[1024,256]{1,0:T(8,128)S(1)} %get-tuple-element.6.refs_2_, s16[2,272,256]{2,1,0:T(8,128)(2,1)S(1)} %collective-permute-done.refs_3_, bf16[48,128,128]{2,1,0:T(8,128)(2,1)} %refs_4_.3), custom_call_target="tpu_custom_call" | custom-call | tf_op jit(solution)/shard_map/visit1/pallas_call | solution.py:186
  33.7 3.7 %collective-permute-start.1 = (s16[2,272,256]{2,1,0:T(8,128)(2,1)S(1)}, s16[2,272,256]{2,1,0:T(8,128)(2,1)S(1)}, u32[]{:S(2)}, u32[]{:S(2)}) collective-permute-start(s16[2,272,256]{2,1,0:T(8,128)(2,1)S(1)} %get-tuple-element.9), channel_id=1, source_target_pairs={{0,504},{8,0},{16,8},{24,16},{32,24},{40,32},{48,40},{56,48},{64,5... | collective-permute-start | bytes 835592 | tf_op jit(solution)/shard_map/ppermute | solution.py:32
  37.4 6.1 %collective-permute-done.1.coded = s16[2,272,256]{2,1,0:T(8,128)(2,1)S(1)} collective-permute-done((s16[2,272,256]{2,1,0:T(8,128)(2,1)S(1)}, s16[2,272,256]{2,1,0:T(8,128)(2,1)S(1)}, u32[]{:S(2)}, u32[]{:S(2)}) %collective-permute-start.1) | collective-permute-done | bytes 278560 | tf_op jit(solution)/shard_map/ppermute | solution.py:32
  43.5 0.9 %unpack.1 = f32[512,256]{1,0:T(8,128)} custom-call(s16[2,272,256]{2,1,0:T(8,128)(2,1)S(1)} %collective-permute-done.1.coded), custom_call_target="tpu_custom_call" | custom-call | tf_op jit(solution)/shard_map/unpack/pallas_call | solution.py:230
Async XLA Ops:
  6.7 20.8 %collective-permute-start = (s16[2,272,256]{2,1,0:T(8,128)(2,1)S(1)}, s16[2,272,256]{2,1,0:T(8,128)(2,1)S(1)}, u32[]{:S(2)}, u32[]{:S(2)}) collective-permute-start(s16[2,272,256]{2,1,0:T(8,128)(2,1)S(1)} %get-tuple-element.7), channel_id=1, source_target_pairs={{0,8},{8,16},{16,24},{24,32},{32,40},{40,48},{48,56},{56,64},{64,7... | collective-permute-start | bytes 835592 | tf_op jit(solution)/shard_map/ppermute | solution.py:32
  33.7 9.8 %collective-permute-start.1 = (s16[2,272,256]{2,1,0:T(8,128)(2,1)S(1)}, s16[2,272,256]{2,1,0:T(8,128)(2,1)S(1)}, u32[]{:S(2)}, u32[]{:S(2)}) collective-permute-start(s16[2,272,256]{2,1,0:T(8,128)(2,1)S(1)} %get-tuple-element.9), channel_id=1, source_target_pairs={{0,504},{8,0},{16,8},{24,16},{32,24},{40,32},{48,40},{56,48},{64,5... | collective-permute-start | bytes 835592 | tf_op jit(solution)/shard_map/ppermute | solution.py:32

commit v2 on v1

v2 whole, which is shorter than its diff:
```python
import jax
import jax.numpy as jnp
from jax import lax
from jax.experimental import pallas as pl
from jax.experimental.pallas import tpu as pltpu
from jax.sharding import PartitionSpec as P

TILE = 128
BATCHES = 2
VISITS = 2
SLOTS = 12
SIDE = 4
PLACES = SIDE * SIDE
ROWS = SIDE * TILE
RANK = 256
HALVES = 2
HALF = ROWS // HALVES
EXTRA = 16
CODED = HALF + EXTRA
ENTRIES = VISITS * BATCHES
NONE = ENTRIES * SLOTS

LEARN = 0.02
DECAY = 0.05
TOP = 32766.0
F32 = jnp.float32
BF16 = jnp.bfloat16


def passed_along(value, axis, steps):
    count = lax.axis_size(axis)
    pairs = [(source, (source + steps) % count) for source in range(count)]
    return lax.ppermute(value, axis, pairs)


def split(value):
    high = value.astype(BF16)
    low = (value - high.astype(F32)).astype(BF16)
    return high, low


def dot(left, right, dims):
    return lax.dot_general(left, right, (dims, ((), ())), preferred_element_type=F32)


def product(left, right, dims):
    (left_dim,), (right_dim,) = dims
    wide = jnp.concatenate([left[0], left[1], left[0]], axis=left_dim)
    tall = jnp.concatenate([right[0], right[0], right[1]], axis=right_dim)
    return dot(wide, tall, dims)


def encode(block):
    peak = jnp.maximum(jnp.max(jnp.abs(block), axis=0, keepdims=True), 1e-30)
    power = jnp.ceil(jnp.log2(peak))
    unit = jnp.exp2(power - 8.0)
    units = jnp.ceil(peak / unit)
    coded = jnp.round(block * (TOP / (units * unit))).astype(jnp.int32)
    row = lax.broadcasted_iota(jnp.int32, (EXTRA, RANK), 0)
    scale = jnp.where(
        row == 0, power.astype(jnp.int32), jnp.where(row == 1, units.astype(jnp.int32), 0)
    )
    return coded.astype(jnp.int16), scale.astype(jnp.int16)


def decode(coded, scale):
    scale = scale.astype(jnp.int32).astype(F32)
    step = scale[1:2] * jnp.exp2(scale[0:1] - 8.0) * (1.0 / TOP)
    return coded.astype(jnp.int32).astype(F32) * step


CHUNK = 512
CHUNKS = ROWS // CHUNK


def visit_batch(observed_tile, users_of, block, store_users):
    block_parts = split(block)
    grad_items = jnp.zeros((ROWS, RANK), F32)
    for chunk in range(CHUNKS):
        old = users_of(chunk)
        parts = split(old)
        predicted = product(parts, block_parts, ((1,), (1,)))
        highs, lows = [], []
        for user_tile in range(CHUNK // TILE):
            high_row, low_row = [], []
            for item_tile in range(SIDE):
                observed = observed_tile(chunk * (CHUNK // TILE) + user_tile, item_tile)
                observed = observed.astype(F32)
                part = predicted[
                    user_tile * TILE : (user_tile + 1) * TILE,
                    item_tile * TILE : (item_tile + 1) * TILE,
                ]
                high, low = split(jnp.where(observed != 0, part - observed, 0.0))
                high_row.append(high)
                low_row.append(low)
            highs.append(jnp.concatenate(high_row, axis=1))
            lows.append(jnp.concatenate(low_row, axis=1))
        left = (jnp.concatenate(highs, axis=0), jnp.concatenate(lows, axis=0))
        grad_users = product(left, block_parts, ((1,), (0,)))
        store_users(chunk, old - LEARN * (grad_users + DECAY * old))
        grad_items = grad_items + product(left, parts, ((0,), (0,)))
    return block - LEARN * (grad_items + DECAY * block)


def chunk_rows(batch, chunk):
    return pl.ds(batch * ROWS + chunk * CHUNK, CHUNK)


def store_coded(block, items_out):
    for half in range(HALVES):
        coded, scale = encode(block[half * HALF : (half + 1) * HALF])
        items_out[half, :HALF] = coded
        items_out[half, HALF:] = scale


def first_kernel(
    lists_in, counts_in, users_in, items_in, ratings_in, users_out, items_out, later_out,
    users, items, tiles, lists, counts, where, sems,
):
    def fetch(source, target, sem):
        return pltpu.make_async_copy(source, target, sems.at[sem])

    item_copy = fetch(items_in, items, 0)
    user_copies = [
        fetch(users_in.at[chunk_rows(batch, chunk)], users.at[chunk_rows(batch, chunk)], 8 + batch * CHUNKS + chunk)
        for batch in range(BATCHES)
        for chunk in range(CHUNKS)
    ]
    tile_copies = [
        fetch(ratings_in.at[pl.ds(entry * SLOTS, SLOTS)], tiles.at[pl.ds(entry * SLOTS, SLOTS)], 1 + entry)
        for entry in range(ENTRIES)
    ]
    list_copy = fetch(lists_in, lists, 5)
    count_copy = fetch(counts_in, counts, 6)
    list_copy.start()
    count_copy.start()
    item_copy.start()
    for batch in range(BATCHES):
        for chunk in range(CHUNKS):
            user_copies[batch * CHUNKS + chunk].start()
        tile_copies[batch].start()
    for entry in range(BATCHES, ENTRIES):
        tile_copies[entry].start()
    tiles[NONE] = jnp.zeros((TILE, TILE), BF16)
    list_copy.wait()
    count_copy.wait()
    for entry in range(ENTRIES):
        for place in range(PLACES):
            where[entry * PLACES + place] = NONE

        def note(slot, carry):
            place = lists[entry, 0, slot] * SIDE + lists[entry, 1, slot]
            where[entry * PLACES + place] = entry * SLOTS + slot
            return carry

        lax.fori_loop(0, counts[entry], note, 0)
    item_copy.wait()
    block = items[...]
    for batch in range(BATCHES):
        for chunk in range(CHUNKS):
            user_copies[batch * CHUNKS + chunk].wait()
        tile_copies[batch].wait()

        def store_users(chunk, rows):
            users_out[chunk_rows(batch, chunk)] = rows

        block = visit_batch(
            lambda row, column: tiles[where[batch * PLACES + row * SIDE + column]],
            lambda chunk: users[chunk_rows(batch, chunk)],
            block,
            store_users,
        )
    store_coded(block, items_out)
    for entry in range(BATCHES, ENTRIES):
        tile_copies[entry].wait()
        for place in range(PLACES):
            later_out[(entry - BATCHES) * PLACES + place] = tiles[where[entry * PLACES + place]]


def second_kernel(users_in, items_in, later_in, users_out, items_out, users, sems):
    block = jnp.concatenate(
        [decode(items_in[half, :HALF], items_in[half, HALF:]) for half in range(HALVES)], axis=0
    )
    copies = []
    for batch in range(BATCHES):

        def store_users(chunk, rows):
            users[chunk_rows(batch, chunk)] = rows
            copies.append(
                pltpu.make_async_copy(
                    users.at[chunk_rows(batch, chunk)],
                    users_out.at[chunk_rows(batch, chunk)],
                    sems.at[len(copies)],
                )
            )
            copies[-1].start()

        block = visit_batch(
            lambda row, column: later_in[batch * PLACES + row * SIDE + column],
            lambda chunk: users_in[chunk_rows(batch, chunk)],
            block,
            store_users,
        )
    store_coded(block, items_out)
    for copy in copies:
        copy.wait()


def held(value):
    return pltpu.with_memory_space_constraint(value, pltpu.HBM)


SPEC_HBM = pl.BlockSpec(memory_space=pltpu.HBM)
SPEC_VMEM = pl.BlockSpec(memory_space=pltpu.VMEM)
PARAMS = pltpu.CompilerParams(vmem_limit_bytes=40 * 1024 * 1024)
CODED_SHAPE = jax.ShapeDtypeStruct((HALVES, CODED, RANK), jnp.int16)
USERS_SHAPE = jax.ShapeDtypeStruct((BATCHES * ROWS, RANK), F32)


def first_call(lists, counts, users, items, ratings):
    return pl.pallas_call(
        first_kernel,
        out_shape=(
            USERS_SHAPE,
            CODED_SHAPE,
            jax.ShapeDtypeStruct((BATCHES * PLACES, TILE, TILE), BF16),
        ),
        in_specs=[SPEC_HBM] * 5,
        out_specs=(SPEC_VMEM,) * 3,
        scratch_shapes=[
            pltpu.VMEM((BATCHES * ROWS, RANK), F32),
            pltpu.VMEM((ROWS, RANK), F32),
            pltpu.VMEM((NONE + 1, TILE, TILE), BF16),
            pltpu.SMEM((ENTRIES, 2, SLOTS), jnp.int32),
            pltpu.SMEM((ENTRIES,), jnp.int32),
            pltpu.SMEM((ENTRIES * PLACES,), jnp.int32),
            pltpu.SemaphoreType.DMA((8 + BATCHES * CHUNKS,)),
        ],
        compiler_params=PARAMS,
        name="first_visit",
    )(held(lists), held(counts), held(users), held(items), held(ratings))


def second_call(users, items, later):
    return pl.pallas_call(
        second_kernel,
        out_shape=(USERS_SHAPE, CODED_SHAPE),
        in_specs=[SPEC_VMEM] * 3,
        out_specs=(SPEC_HBM, SPEC_VMEM),
        scratch_shapes=[
            pltpu.VMEM((BATCHES * ROWS, RANK), F32),
            pltpu.SemaphoreType.DMA((BATCHES * CHUNKS,)),
        ],
        compiler_params=PARAMS,
        name="second_visit",
    )(users, items, later)


def decode_kernel(coded, items):
    for half in range(HALVES):
        items[half * HALF : (half + 1) * HALF] = decode(coded[half, :HALF], coded[half, HALF:])


def decode_call(coded):
    spec_vmem = pl.BlockSpec(memory_space=pltpu.VMEM)
    return pl.pallas_call(
        decode_kernel,
        out_shape=jax.ShapeDtypeStruct((ROWS, RANK), F32),
        in_specs=[spec_vmem],
        out_specs=spec_vmem,
        compiler_params=pltpu.CompilerParams(vmem_limit_bytes=8 * 1024 * 1024),
        name="unpack",
    )(coded)


def on_device(user_factors, item_factors, ratings, tile_lists, tile_counts):
    users, coded, later = first_call(
        tile_lists, tile_counts, user_factors, item_factors, ratings
    )
    users, coded = second_call(users, passed_along(coded, "blk", 1), later)
    items = decode_call(passed_along(coded, "blk", -1))
    return (users, items)


def solution(mesh):
    in_specs = (
        P(("grp", "blk"), None),
        P(("grp", "blk"), None),
        P(("grp", "blk"), None, None),
        P(("grp", "blk"), None, None),
        P(("grp", "blk")),
    )
    out_specs = (P(("grp", "blk"), None), P(("grp", "blk"), None))
    return jax.shard_map(
        on_device, mesh=mesh, in_specs=in_specs, out_specs=out_specs, check_vma=False
    )
```

time: 44.6 us -> 40.8 us (0.915)
  Pallas kernels: 13.1 us -> 9.48 us
    pallas_call x2, Pallas kernels: 12.3 us -> 8.63 us  [the longest x1 4.76 us: first_call(): pl.pallas_call(first_kernel, out_shape=(USERS_SHAPE, CODED_SHAPE, jax.Sha...]
where the time goes in v2:
time: 40.8 us; the launch traced here: 40.7 us
  waiting for transfers between devices  22.6 us (55%)
  Pallas kernels  9.48 us (23%)
  starting transfers between devices  7.93 us (19%)
  between operations  0.66 us (2%)
    ppermute x2, waiting for transfers between devices, passed_along(): return lax.ppermute(value, axis, pairs)  22.6 us
    ppermute x2, starting transfers between devices, passed_along(): return lax.ppermute(value, axis, pairs)  7.93 us
    pallas_call x1, Pallas kernels, first_call(): pl.pallas_call(first_kernel, out_shape=(USERS_SHAPE, CODED_SHAPE, jax.Sha...  4.76 us
    pallas_call x1, Pallas kernels, second_call(): pl.pallas_call(second_kernel, out_shape=(USERS_SHAPE, CODED_SHAPE), in_sp...  3.86 us
    pallas_call x1, Pallas kernels, decode_call(): pl.pallas_call(decode_kernel, out_shape=jax.ShapeDtypeStruct((ROWS, RANK)...  0.85 us
  transfers between devices with their start and end apart: 2, of which 2 were waited for; matrix products, arithmetic and copies ran while one was open for 0% of the time, Pallas kernels for 0%

profile of v2, /device:TPU:16, one launch (start us, length us, event | category | flops | bytes accessed | tf_op | source)
XLA Modules:
  0.0 40.7 jit_solution(9293150559740857667)
XLA Ops:
  0.6 4.8 %first_visit.1 = (f32[1024,256]{1,0:T(8,128)S(1)}, s16[2,272,256]{2,1,0:T(8,128)(2,1)S(1)}, bf16[32,128,128]{2,1,0:T(8,128)(2,1)S(1)}) custom-call(s32[4,2,12]{2,1,0:T(2,128)} %lists_in.1, s32[4]{0:T(128)} %counts_in.1, f32[1024,256]{1,0:T(8,128)} %users_in.1, f32[512,256]{1,0:T(8,128)} %items_in.1, bf16[48,128,128]{2,1,0:T(8,128)(2,1)} %ratings_in.1), custom_call_target="tpu_custom_call" | custom-call | tf_op jit(solution)/shard_map/first_visit/pallas_call | solution.py:221
  5.4 4.3 %collective-permute-start = (s16[2,272,256]{2,1,0:T(8,128)(2,1)S(1)}, s16[2,272,256]{2,1,0:T(8,128)(2,1)S(1)}, u32[]{:S(2)}, u32[]{:S(2)}) collective-permute-start(s16[2,272,256]{2,1,0:T(8,128)(2,1)S(1)} %get-tuple-element.8), channel_id=1, source_target_pairs={{0,8},{8,16},{16,24},{24,32},{32,40},{40,48},{48,56},{56,64},{64,7... | collective-permute-start | bytes 835592 | tf_op jit(solution)/shard_map/ppermute | solution.py:33
  9.7 16.5 %collective-permute-done.items_in = s16[2,272,256]{2,1,0:T(8,128)(2,1)S(1)} collective-permute-done((s16[2,272,256]{2,1,0:T(8,128)(2,1)S(1)}, s16[2,272,256]{2,1,0:T(8,128)(2,1)S(1)}, u32[]{:S(2)}, u32[]{:S(2)}) %collective-permute-start) | collective-permute-done | bytes 278560 | tf_op jit(solution)/shard_map/ppermute | solution.py:33
  26.2 3.9 %second_visit.1 = (f32[1024,256]{1,0:T(8,128)}, s16[2,272,256]{2,1,0:T(8,128)(2,1)S(1)}) custom-call(f32[1024,256]{1,0:T(8,128)S(1)} %get-tuple-element.7.users_in, s16[2,272,256]{2,1,0:T(8,128)(2,1)S(1)} %collective-permute-done.items_in, bf16[32,128,128]{2,1,0:T(8,128)(2,1)S(1)} %get-tuple-element.9.later_in), custom_call_target="tpu_custom_call" | custom-call | tf_op jit(solution)/shard_map/second_visit/pallas_call | solution.py:245
  30.1 3.6 %collective-permute-start.1 = (s16[2,272,256]{2,1,0:T(8,128)(2,1)S(1)}, s16[2,272,256]{2,1,0:T(8,128)(2,1)S(1)}, u32[]{:S(2)}, u32[]{:S(2)}) collective-permute-start(s16[2,272,256]{2,1,0:T(8,128)(2,1)S(1)} %get-tuple-element.11), channel_id=1, source_target_pairs={{0,504},{8,0},{16,8},{24,16},{32,24},{40,32},{48,40},{56,48},{64,5... | collective-permute-start | bytes 835592 | tf_op jit(solution)/shard_map/ppermute | solution.py:33
  33.7 6.1 %collective-permute-done.1.coded = s16[2,272,256]{2,1,0:T(8,128)(2,1)S(1)} collective-permute-done((s16[2,272,256]{2,1,0:T(8,128)(2,1)S(1)}, s16[2,272,256]{2,1,0:T(8,128)(2,1)S(1)}, u32[]{:S(2)}, u32[]{:S(2)}) %collective-permute-start.1) | collective-permute-done | bytes 278560 | tf_op jit(solution)/shard_map/ppermute | solution.py:33
  39.8 0.9 %unpack.1 = f32[512,256]{1,0:T(8,128)} custom-call(s16[2,272,256]{2,1,0:T(8,128)(2,1)S(1)} %collective-permute-done.1.coded), custom_call_target="tpu_custom_call" | custom-call | tf_op jit(solution)/shard_map/unpack/pallas_call | solution.py:266
Async XLA Ops:
  5.4 20.8 %collective-permute-start = (s16[2,272,256]{2,1,0:T(8,128)(2,1)S(1)}, s16[2,272,256]{2,1,0:T(8,128)(2,1)S(1)}, u32[]{:S(2)}, u32[]{:S(2)}) collective-permute-start(s16[2,272,256]{2,1,0:T(8,128)(2,1)S(1)} %get-tuple-element.8), channel_id=1, source_target_pairs={{0,8},{8,16},{16,24},{24,32},{32,40},{40,48},{48,56},{56,64},{64,7... | collective-permute-start | bytes 835592 | tf_op jit(solution)/shard_map/ppermute | solution.py:33
  30.1 9.7 %collective-permute-start.1 = (s16[2,272,256]{2,1,0:T(8,128)(2,1)S(1)}, s16[2,272,256]{2,1,0:T(8,128)(2,1)S(1)}, u32[]{:S(2)}, u32[]{:S(2)}) collective-permute-start(s16[2,272,256]{2,1,0:T(8,128)(2,1)S(1)} %get-tuple-element.11), channel_id=1, source_target_pairs={{0,504},{8,0},{16,8},{24,16},{32,24},{40,32},{48,40},{56,48},{64,5... | collective-permute-start | bytes 835592 | tf_op jit(solution)/shard_map/ppermute | solution.py:33

commit v3 on v0

v3 whole, which is shorter than its diff:
```python
import jax
import jax.numpy as jnp
from jax import lax
from jax.experimental import pallas as pl
from jax.experimental.pallas import tpu as pltpu
from jax.sharding import PartitionSpec as P

TILE = 128
BATCHES = 2
VISITS = 2
SLOTS = 12
SIDE = 4
PLACES = SIDE * SIDE
ROWS = SIDE * TILE
RANK = 256
HALVES = 2
HALF = ROWS // HALVES
EXTRA = 16
CODED = HALF + EXTRA
ENTRIES = VISITS * BATCHES
LISTED = BATCHES * SLOTS

LEARN = 0.02
DECAY = 0.05
TOP = 32766.0
F32 = jnp.float32
BF16 = jnp.bfloat16


def passed_along(value, axis, steps):
    count = lax.axis_size(axis)
    pairs = [(source, (source + steps) % count) for source in range(count)]
    return lax.ppermute(value, axis, pairs)


def split(value):
    high = value.astype(BF16)
    low = (value - high.astype(F32)).astype(BF16)
    return high, low


def dot(left, right, dims):
    return lax.dot_general(left, right, (dims, ((), ())), preferred_element_type=F32)


def product(left, right, dims):
    (left_dim,), (right_dim,) = dims
    wide = jnp.concatenate([left[0], left[1], left[0]], axis=left_dim)
    tall = jnp.concatenate([right[0], right[0], right[1]], axis=right_dim)
    return dot(wide, tall, dims)


def encode(block):
    peak = jnp.maximum(jnp.max(jnp.abs(block), axis=0, keepdims=True), 1e-30)
    power = jnp.ceil(jnp.log2(peak))
    unit = jnp.exp2(power - 8.0)
    units = jnp.ceil(peak / unit)
    coded = jnp.round(block * (TOP / (units * unit))).astype(jnp.int32)
    row = lax.broadcasted_iota(jnp.int32, (EXTRA, RANK), 0)
    scale = jnp.where(
        row == 0, power.astype(jnp.int32), jnp.where(row == 1, units.astype(jnp.int32), 0)
    )
    return coded.astype(jnp.int16), scale.astype(jnp.int16)


def decode(coded, scale):
    scale = scale.astype(jnp.int32).astype(F32)
    step = scale[1:2] * jnp.exp2(scale[0:1] - 8.0) * (1.0 / TOP)
    return coded.astype(jnp.int32).astype(F32) * step


def batch_rows(batch):
    return pl.ds(batch * ROWS, ROWS)


ORDER = "P00 P10 R00 R10 G00 G10 P01 P11 R01 R11 G01 G11"


def block_steps(observed_tile, users_of, halves, residues_out, blocks_out, before=None):
    parts, predicted, residues = {}, {}, {}
    columns = SIDE // HALVES
    for item in ORDER.split():
        kind, half, batch = item[0], int(item[1]), int(item[2])
        span = pl.ds(half * HALF, HALF)
        if before is not None:
            before(kind, half, batch)
        if kind == "P":
            parts[half] = split(halves[half])
            for which in range(2):
                blocks_out[batch, which, span] = parts[half][which]
            predicted[half] = product(users_of(batch), parts[half], ((1,), (1,)))
        elif kind == "R":
            highs, lows = [], []
            for row in range(SIDE):
                high_row, low_row = [], []
                for column in range(columns):
                    observed = observed_tile(batch, row * SIDE + half * columns + column)
                    observed = observed.astype(F32)
                    part = predicted[half][
                        row * TILE : (row + 1) * TILE, column * TILE : (column + 1) * TILE
                    ]
                    high, low = split(jnp.where(observed != 0, part - observed, 0.0))
                    high_row.append(high)
                    low_row.append(low)
                highs.append(jnp.concatenate(high_row, axis=1))
                lows.append(jnp.concatenate(low_row, axis=1))
            residues[half] = (jnp.concatenate(highs, axis=0), jnp.concatenate(lows, axis=0))
            for which in range(2):
                residues_out[batch, which, :, span] = residues[half][which]
        else:
            grad_items = product(residues[half], users_of(batch), ((0,), (0,)))
            halves[half] = halves[half] - LEARN * (grad_items + DECAY * halves[half])


def users_step(old, residues, blocks, batch):
    grad_users = product(
        (residues[batch, 0], residues[batch, 1]), (blocks[batch, 0], blocks[batch, 1]), ((1,), (0,))
    )
    return old - LEARN * (grad_users + DECAY * old)


def store_coded(halves, items_out):
    for half in range(HALVES):
        coded, scale = encode(halves[half])
        items_out[half, :HALF] = coded
        items_out[half, HALF:] = scale


def place_slots(where, lists, counts, visit):
    for batch in range(BATCHES):
        entry = visit * BATCHES + batch
        base = batch * (PLACES + 1)
        count = counts[entry]
        for place in range(PLACES):
            where[base + place] = LISTED
        for slot in range(SLOTS):
            row = jnp.clip(lists[entry, 0, slot], 0, SIDE - 1)
            column = jnp.clip(lists[entry, 1, slot], 0, SIDE - 1)
            live = slot < count
            where[base + jnp.where(live, row * SIDE + column, PLACES)] = batch * SLOTS + slot


def fetch_lists(lists_in, counts_in, lists, counts, sems):
    copies = (
        pltpu.make_async_copy(lists_in, lists, sems.at[0]),
        pltpu.make_async_copy(counts_in, counts, sems.at[1]),
    )
    for copy in copies:
        copy.start()
    return copies


def fetch_tiles(ratings_in, tiles, visit, batch, sem):
    first = (visit * BATCHES + batch) * SLOTS
    copy = pltpu.make_async_copy(
        ratings_in.at[pl.ds(first, SLOTS)], tiles.at[pl.ds(batch * SLOTS, SLOTS)], sem
    )
    copy.start()
    return copy


def first_block_kernel(
    lists_in, counts_in, users_in, items_in, ratings_in,
    users, items_out, residues_out, blocks_out,
    items, tiles, lists, counts, where, sems,
):
    list_copies = fetch_lists(lists_in, counts_in, lists, counts, sems)
    copies = []

    def pieces(source, target, first, size, count):
        for piece in range(count):
            rows = pl.ds(first + piece * (size // count), size // count)
            copies.append(
                pltpu.make_async_copy(source.at[rows], target.at[rows], sems.at[2 + len(copies)])
            )
            copies[-1].start()

    pieces(items_in, items, 0, ROWS, 1)
    waits = []
    for batch in range(BATCHES):
        pieces(users_in, users, batch * ROWS, ROWS, 1)
        pieces(ratings_in, tiles, batch * SLOTS, SLOTS, 1)
        waits.append(len(copies))
    tiles[LISTED] = jnp.zeros((TILE, TILE), BF16)
    for copy in list_copies:
        copy.wait()
    place_slots(where, lists, counts, 0)
    halves = [None] * HALVES
    user_parts = {}

    def users_of(batch):
        if batch not in user_parts:
            user_parts[batch] = split(users[batch_rows(batch)])
        return user_parts[batch]

    def before(kind, half, batch):
        if kind == "P" and half == 0 and batch == 0:
            for copy in copies[: waits[0]]:
                copy.wait()
        if kind == "P" and batch == 0:
            halves[half] = items[half * HALF : (half + 1) * HALF]
        if kind == "P" and half == 0 and batch == 1:
            for copy in copies[waits[0] :]:
                copy.wait()

    block_steps(
        lambda batch, place: tiles[where[batch * (PLACES + 1) + place]],
        users_of,
        halves,
        residues_out,
        blocks_out,
        before,
    )
    store_coded(halves, items_out)


def first_users_kernel(
    lists_in, counts_in, ratings_in, users, residues, blocks,
    users_out, parts_out, later_out,
    tiles, lists, counts, where, sems,
):
    list_copies = fetch_lists(lists_in, counts_in, lists, counts, sems)
    tile_copies = [
        fetch_tiles(ratings_in, tiles, 1, batch, sems.at[2 + batch]) for batch in range(BATCHES)
    ]
    tiles[LISTED] = jnp.zeros((TILE, TILE), BF16)
    for batch in range(BATCHES):
        rows = batch_rows(batch)
        new = users_step(users[rows], residues, blocks, batch)
        users_out[rows] = new
        parts_out[0, rows], parts_out[1, rows] = split(new)
    for copy in list_copies:
        copy.wait()
    for copy in tile_copies:
        copy.wait()
    place_slots(where, lists, counts, 1)
    for batch in range(BATCHES):
        for place in range(PLACES):
            later_out[batch * PLACES + place] = tiles[where[batch * (PLACES + 1) + place]]


def second_block_kernel(parts, items_in, later, items_out, residues_out, blocks_out):
    halves = [decode(items_in[half, :HALF], items_in[half, HALF:]) for half in range(HALVES)]
    block_steps(
        lambda batch, place: later[batch * PLACES + place],
        lambda batch: (parts[0, batch_rows(batch)], parts[1, batch_rows(batch)]),
        halves,
        residues_out,
        blocks_out,
    )
    store_coded(halves, items_out)


def second_users_kernel(users, residues, blocks, users_out, fresh, sems):
    copies = []
    for batch in range(BATCHES):
        rows = batch_rows(batch)
        fresh[rows] = users_step(users[rows], residues, blocks, batch)
        copies.append(
            pltpu.make_async_copy(fresh.at[rows], users_out.at[rows], sems.at[batch])
        )
        copies[-1].start()
    for copy in copies:
        copy.wait()


def held(value):
    return pltpu.with_memory_space_constraint(value, pltpu.HBM)


SPEC_HBM = pl.BlockSpec(memory_space=pltpu.HBM)
SPEC_VMEM = pl.BlockSpec(memory_space=pltpu.VMEM)
CODED_SHAPE = jax.ShapeDtypeStruct((HALVES, CODED, RANK), jnp.int16)
USERS_SHAPE = jax.ShapeDtypeStruct((BATCHES * ROWS, RANK), F32)
PARTS_SHAPE = jax.ShapeDtypeStruct((2, BATCHES * ROWS, RANK), BF16)
LATER_SHAPE = jax.ShapeDtypeStruct((BATCHES * PLACES, TILE, TILE), BF16)
RESIDUES_SHAPE = jax.ShapeDtypeStruct((BATCHES, 2, ROWS, ROWS), BF16)
BLOCKS_SHAPE = jax.ShapeDtypeStruct((BATCHES, 2, ROWS, RANK), BF16)
PRODUCT_FLOPS = 2 * 3 * BATCHES * ROWS * ROWS * RANK


def call(kernel, name, outs, out_specs, in_specs, scratch, products, args):
    return pl.pallas_call(
        kernel,
        out_shape=outs,
        in_specs=in_specs,
        out_specs=out_specs,
        scratch_shapes=scratch,
        compiler_params=pltpu.CompilerParams(vmem_limit_bytes=28 * 1024 * 1024),
        cost_estimate=pl.CostEstimate(
            flops=products * PRODUCT_FLOPS, bytes_accessed=1 << 20, transcendentals=0
        ),
        name=name,
    )(*args)


def list_scratch():
    return [
        pltpu.VMEM((LISTED + 1, TILE, TILE), BF16),
        pltpu.SMEM((ENTRIES, 2, SLOTS), jnp.int32),
        pltpu.SMEM((ENTRIES,), jnp.int32),
        pltpu.SMEM((BATCHES * (PLACES + 1),), jnp.int32),
    ]


def first_block(lists, counts, users, items, ratings):
    return call(
        first_block_kernel,
        "first_block",
        (USERS_SHAPE, CODED_SHAPE, RESIDUES_SHAPE, BLOCKS_SHAPE),
        (SPEC_VMEM,) * 4,
        [SPEC_HBM] * 5,
        [pltpu.VMEM((ROWS, RANK), F32), *list_scratch(), pltpu.SemaphoreType.DMA((7,))],
        2,
        (held(lists), held(counts), held(users), held(items), held(ratings)),
    )


def first_users(lists, counts, ratings, users, residues, blocks):
    return call(
        first_users_kernel,
        "first_users",
        (USERS_SHAPE, PARTS_SHAPE, LATER_SHAPE),
        (SPEC_VMEM,) * 3,
        [SPEC_HBM] * 3 + [SPEC_VMEM] * 3,
        [*list_scratch(), pltpu.SemaphoreType.DMA((4,))],
        1,
        (held(lists), held(counts), held(ratings), users, residues, blocks),
    )


def second_block(parts, items, later):
    return call(
        second_block_kernel,
        "second_block",
        (CODED_SHAPE, RESIDUES_SHAPE, BLOCKS_SHAPE),
        (SPEC_VMEM,) * 3,
        [SPEC_VMEM] * 3,
        [],
        2,
        (parts, items, later),
    )


def second_users(users, residues, blocks):
    return call(
        second_users_kernel,
        "second_users",
        USERS_SHAPE,
        SPEC_HBM,
        [SPEC_VMEM] * 3,
        [pltpu.VMEM((BATCHES * ROWS, RANK), F32), pltpu.SemaphoreType.DMA((BATCHES,))],
        1,
        (users, residues, blocks),
    )


PIECE = 128


def unpack_kernel(coded, items_out, items, sems):
    copies = []
    for piece in range(ROWS // PIECE):
        half, first = divmod(piece * PIECE, HALF)
        rows = pl.ds(piece * PIECE, PIECE)
        items[rows] = decode(coded[half, first : first + PIECE], coded[half, HALF:])
        copies.append(pltpu.make_async_copy(items.at[rows], items_out.at[rows], sems.at[piece]))
        copies[-1].start()
    for copy in copies:
        copy.wait()


def unpack(coded):
    return pl.pallas_call(
        unpack_kernel,
        out_shape=jax.ShapeDtypeStruct((ROWS, RANK), F32),
        in_specs=[SPEC_VMEM],
        out_specs=SPEC_HBM,
        scratch_shapes=[
            pltpu.VMEM((ROWS, RANK), F32),
            pltpu.SemaphoreType.DMA((ROWS // PIECE,)),
        ],
        compiler_params=pltpu.CompilerParams(vmem_limit_bytes=8 * 1024 * 1024),
        name="unpack",
    )(coded)


def on_device(user_factors, item_factors, ratings, tile_lists, tile_counts):
    users, coded, residues, blocks = first_block(
        tile_lists, tile_counts, user_factors, item_factors, ratings
    )
    arrived = passed_along(coded, "blk", 1)
    users, parts, later = first_users(tile_lists, tile_counts, ratings, users, residues, blocks)
    coded, residues, blocks = second_block(parts, arrived, later)
    returned = passed_along(coded, "blk", -1)
    users = second_users(users, residues, blocks)
    items = unpack(returned)
    return (users, items)


def solution(mesh):
    in_specs = (
        P(("grp", "blk"), None),
        P(("grp", "blk"), None),
        P(("grp", "blk"), None, None),
        P(("grp", "blk"), None, None),
        P(("grp", "blk")),
    )
    out_specs = (P(("grp", "blk"), None), P(("grp", "blk"), None))
    return jax.shard_map(
        on_device, mesh=mesh, in_specs=in_specs, out_specs=out_specs, check_vma=False
    )
```

time: 413 us -> 38.9 us (0.09)
  the two profiles are of different devices: /device:TPU:79 before, /device:TPU:16 now
where the time goes in v3:
time: 38.9 us; the launch traced here: 38.7 us
  waiting for transfers between devices  19.2 us (49%)
  Pallas kernels  10.9 us (28%)
  starting transfers between devices  7.93 us (20%)
  between operations  0.68 us (2%)
    ppermute x2, waiting for transfers between devices, passed_along(): return lax.ppermute(value, axis, pairs)  19.2 us
    pallas_call x4, Pallas kernels, call(): pl.pallas_call(kernel, out_shape=outs, in_specs=in_specs, out_specs=out_s...  10.1 us
    ppermute x2, starting transfers between devices, passed_along(): return lax.ppermute(value, axis, pairs)  7.93 us
    pallas_call x1, Pallas kernels, unpack(): pl.pallas_call(unpack_kernel, out_shape=jax.ShapeDtypeStruct((ROWS, RANK)...  0.84 us
  transfers between devices with their start and end apart: 2, of which 2 were waited for; matrix products, arithmetic and copies ran while one was open for 0% of the time, Pallas kernels for 9%

profile of v3, /device:TPU:16, one launch (start us, length us, event | category | flops | bytes accessed | tf_op | source)
XLA Modules:
  0.0 38.7 jit_solution(14199144567339390650)
XLA Ops:
  0.6 4.1 %first_block.1 = (f32[1024,256]{1,0:T(8,128)S(1)}, s16[2,272,256]{2,1,0:T(8,128)(2,1)S(1)}, bf16[2,2,512,512]{3,2,1,0:T(8,128)(2,1)S(1)}, bf16[2,2,512,256]{3,2,1,0:T(8,128)(2,1)S(1)}) custom-call(s32[4,2,12]{2,1,0:T(2,128)} %lists_in.3, s32[4]{0:T(128)} %counts_in.3, f32[1024,256]{1,0:T(8,128)} %users_in.1, f32[512,256]{1,0:T(8,128)} %items_in.1, ...), custom_call_target="tpu_custom_call" | custom-call | flops 1610612736 | bytes 1048576 | tf_op jit(solution)/shard_map/first_block/pallas_call | solution.py:283
  4.7 4.3 %collective-permute-start = (s16[2,272,256]{2,1,0:T(8,128)(2,1)S(1)}, s16[2,272,256]{2,1,0:T(8,128)(2,1)S(1)}, u32[]{:S(2)}, u32[]{:S(2)}) collective-permute-start(s16[2,272,256]{2,1,0:T(8,128)(2,1)S(1)} %get-tuple-element.17), channel_id=1, source_target_pairs={{0,8},{8,16},{16,24},{24,32},{32,40},{40,48},{48,56},{56,64},{64,7... | collective-permute-start | bytes 835592 | tf_op jit(solution)/shard_map/ppermute | solution.py:33
  9.0 1.4 %first_users.1 = (f32[1024,256]{1,0:T(8,128)S(1)}, bf16[2,1024,256]{2,1,0:T(8,128)(2,1)S(1)}, bf16[32,128,128]{2,1,0:T(8,128)(2,1)S(1)}) custom-call(s32[4,2,12]{2,1,0:T(2,128)} %lists_in.3, s32[4]{0:T(128)} %counts_in.3, bf16[48,128,128]{2,1,0:T(8,128)(2,1)} %ratings_in.3, f32[1024,256]{1,0:T(8,128)S(1)} %get-tuple-element.12.users, ...), custom_call_target="tpu_custom_call" | custom-call | flops 805306368 | bytes 1048576 | tf_op jit(solution)/shard_map/first_users/pallas_call | solution.py:283
  10.4 15.1 %collective-permute-done.items_in = s16[2,272,256]{2,1,0:T(8,128)(2,1)S(1)} collective-permute-done((s16[2,272,256]{2,1,0:T(8,128)(2,1)S(1)}, s16[2,272,256]{2,1,0:T(8,128)(2,1)S(1)}, u32[]{:S(2)}, u32[]{:S(2)}) %collective-permute-start) | collective-permute-done | bytes 278560 | tf_op jit(solution)/shard_map/ppermute | solution.py:33
  25.5 2.6 %second_block.1 = (s16[2,272,256]{2,1,0:T(8,128)(2,1)S(1)}, bf16[2,2,512,512]{3,2,1,0:T(8,128)(2,1)S(1)}, bf16[2,2,512,256]{3,2,1,0:T(8,128)(2,1)S(1)}) custom-call(bf16[2,1024,256]{2,1,0:T(8,128)(2,1)S(1)} %get-tuple-element.16.parts, s16[2,272,256]{2,1,0:T(8,128)(2,1)S(1)} %collective-permute-done.items_in, bf16[32,128,128]{2,1,0:T(8,128)(2,1)S(1)} %get-tuple-element.18.later), custom_call_target="tpu_custom_call" | custom-call | flops 1610612736 | bytes 1048576 | tf_op jit(solution)/shard_map/second_block/pallas_call | solution.py:283
  28.1 3.6 %collective-permute-start.1 = (s16[2,272,256]{2,1,0:T(8,128)(2,1)S(1)}, s16[2,272,256]{2,1,0:T(8,128)(2,1)S(1)}, u32[]{:S(2)}, u32[]{:S(2)}) collective-permute-start(s16[2,272,256]{2,1,0:T(8,128)(2,1)S(1)} %get-tuple-element.21), channel_id=1, source_target_pairs={{0,504},{8,0},{16,8},{24,16},{32,24},{40,32},{48,40},{56,48},{64,5... | collective-permute-start | bytes 835592 | tf_op jit(solution)/shard_map/ppermute | solution.py:33
  31.8 2.0 %second_users.1 = f32[1024,256]{1,0:T(8,128)} custom-call(f32[1024,256]{1,0:T(8,128)S(1)} %get-tuple-element.15.users, bf16[2,2,512,512]{3,2,1,0:T(8,128)(2,1)S(1)} %get-tuple-element.19.residues, bf16[2,2,512,256]{3,2,1,0:T(8,128)(2,1)S(1)} %get-tuple-element.20.blocks), custom_call_target="tpu_custom_call" | custom-call | flops 805306368 | bytes 1048576 | tf_op jit(solution)/shard_map/second_users/pallas_call | solution.py:283
  33.8 4.1 %collective-permute-done.1.coded = s16[2,272,256]{2,1,0:T(8,128)(2,1)S(1)} collective-permute-done((s16[2,272,256]{2,1,0:T(8,128)(2,1)S(1)}, s16[2,272,256]{2,1,0:T(8,128)(2,1)S(1)}, u32[]{:S(2)}, u32[]{:S(2)}) %collective-permute-start.1) | collective-permute-done | bytes 278560 | tf_op jit(solution)/shard_map/ppermute | solution.py:33
  37.9 0.8 %unpack.1 = f32[512,256]{1,0:T(8,128)} custom-call(s16[2,272,256]{2,1,0:T(8,128)(2,1)S(1)} %collective-permute-done.1.coded), custom_call_target="tpu_custom_call" | custom-call | tf_op jit(solution)/shard_map/unpack/pallas_call | solution.py:374
Async XLA Ops:
  4.7 20.8 %collective-permute-start = (s16[2,272,256]{2,1,0:T(8,128)(2,1)S(1)}, s16[2,272,256]{2,1,0:T(8,128)(2,1)S(1)}, u32[]{:S(2)}, u32[]{:S(2)}) collective-permute-start(s16[2,272,256]{2,1,0:T(8,128)(2,1)S(1)} %get-tuple-element.17), channel_id=1, source_target_pairs={{0,8},{8,16},{16,24},{24,32},{32,40},{40,48},{48,56},{56,64},{64,7... | collective-permute-start | bytes 835592 | tf_op jit(solution)/shard_map/ppermute | solution.py:33
  28.1 9.7 %collective-permute-start.1 = (s16[2,272,256]{2,1,0:T(8,128)(2,1)S(1)}, s16[2,272,256]{2,1,0:T(8,128)(2,1)S(1)}, u32[]{:S(2)}, u32[]{:S(2)}) collective-permute-start(s16[2,272,256]{2,1,0:T(8,128)(2,1)S(1)} %get-tuple-element.21), channel_id=1, source_target_pairs={{0,504},{8,0},{16,8},{24,16},{32,24},{40,32},{48,40},{56,48},{64,5... | collective-permute-start | bytes 835592 | tf_op jit(solution)/shard_map/ppermute | solution.py:33

commit v4 on v3

v4 whole, which is shorter than its diff:
```python
import jax
import jax.numpy as jnp
from jax import lax
from jax.experimental import pallas as pl
from jax.experimental.pallas import tpu as pltpu
from jax.sharding import PartitionSpec as P

TILE = 128
BATCHES = 2
VISITS = 2
SLOTS = 12
SIDE = 4
PLACES = SIDE * SIDE
ROWS = SIDE * TILE
RANK = 256
HALVES = 2
HALF = ROWS // HALVES
EXTRA = 16
ENTRIES = VISITS * BATCHES
LISTED = BATCHES * SLOTS
NONE = ENTRIES * SLOTS

LEARN = 0.02
DECAY = 0.05
TOP = 32766.0
F32 = jnp.float32
BF16 = jnp.bfloat16


def passed_along(value, axis, steps):
    count = lax.axis_size(axis)
    pairs = [(source, (source + steps) % count) for source in range(count)]
    return lax.ppermute(value, axis, pairs)


def split(value):
    high = value.astype(BF16)
    low = (value - high.astype(F32)).astype(BF16)
    return high, low


def dot(left, right, dims):
    return lax.dot_general(left, right, (dims, ((), ())), preferred_element_type=F32)


def product(left, right, dims):
    (left_dim,), (right_dim,) = dims
    wide = jnp.concatenate([left[0], left[1], left[0]], axis=left_dim)
    tall = jnp.concatenate([right[0], right[0], right[1]], axis=right_dim)
    return dot(wide, tall, dims)


def encode(block):
    peak = jnp.maximum(jnp.max(jnp.abs(block), axis=0, keepdims=True), 1e-30)
    power = jnp.ceil(jnp.log2(peak))
    unit = jnp.exp2(power - 8.0)
    units = jnp.ceil(peak / unit)
    coded = jnp.round(block * (TOP / (units * unit))).astype(jnp.int32)
    return coded.astype(jnp.int16), (power.astype(jnp.int32), units.astype(jnp.int32))


def decode(coded, half, first=0, size=HALF):
    scale = coded[ROWS:].astype(jnp.int32).astype(F32)
    power, units = scale[2 * half : 2 * half + 1], scale[2 * half + 1 : 2 * half + 2]
    step = units * jnp.exp2(power - 8.0) * (1.0 / TOP)
    start = half * HALF + first
    return coded[start : start + size].astype(jnp.int32).astype(F32) * step


def batch_rows(batch):
    return pl.ds(batch * ROWS, ROWS)


def residue_parts(predicted, observed_tile, columns):
    highs, lows = [], []
    for row in range(SIDE):
        high_row, low_row = [], []
        for column in range(columns):
            observed = observed_tile(row, column).astype(F32)
            part = predicted[row * TILE : (row + 1) * TILE, column * TILE : (column + 1) * TILE]
            high, low = split(jnp.where(observed != 0, part - observed, 0.0))
            high_row.append(high)
            low_row.append(low)
        highs.append(jnp.concatenate(high_row, axis=1))
        lows.append(jnp.concatenate(low_row, axis=1))
    return jnp.concatenate(highs, axis=0), jnp.concatenate(lows, axis=0)


ORDER = "P00 P10 R00 R10 G00 G10 P01 P11 R01 R11 G01 G11"


def block_steps(observed_tile, users_of, halves, blocks_out, before=None):
    parts, predicted, residues = {}, {}, {}
    columns = SIDE // HALVES
    for item in ORDER.split():
        kind, half, batch = item[0], int(item[1]), int(item[2])
        span = pl.ds(half * HALF, HALF)
        if before is not None:
            before(kind, half, batch)
        if kind == "P":
            parts[half] = split(halves[half])
            for which in range(2):
                blocks_out[batch, which, span] = parts[half][which]
            predicted[half] = product(users_of(batch), parts[half], ((1,), (1,)))
        elif kind == "R":
            residues[half] = residue_parts(
                predicted[half],
                lambda row, column: observed_tile(batch, row * SIDE + half * columns + column),
                columns,
            )
        else:
            grad_items = product(residues[half], users_of(batch), ((0,), (0,)))
            halves[half] = halves[half] - LEARN * (grad_items + DECAY * halves[half])


def users_step(old, parts, block, observed_tile):
    predicted = product(parts, block, ((1,), (1,)))
    residues = residue_parts(
        predicted, lambda row, column: observed_tile(row * SIDE + column), SIDE
    )
    grad_users = product(residues, block, ((1,), (0,)))
    return old - LEARN * (grad_users + DECAY * old)


def store_coded(halves, items_out):
    row = lax.broadcasted_iota(jnp.int32, (EXTRA, RANK), 0)
    scales = jnp.zeros((EXTRA, RANK), jnp.int32)
    for half in range(HALVES):
        coded, scale = encode(halves[half])
        items_out[half * HALF : (half + 1) * HALF] = coded
        for which in range(2):
            scales = jnp.where(row == 2 * half + which, scale[which], scales)
    items_out[ROWS:] = scales.astype(jnp.int16)


def place_slots(where, lists, counts, visit, first, none):
    for batch in range(BATCHES):
        entry = visit * BATCHES + batch
        base = (first + batch) * (PLACES + 1)
        count = counts[entry]
        for place in range(PLACES):
            where[base + place] = none
        for slot in range(SLOTS):
            row = jnp.clip(lists[entry, 0, slot], 0, SIDE - 1)
            column = jnp.clip(lists[entry, 1, slot], 0, SIDE - 1)
            target = jnp.where(slot < count, row * SIDE + column, PLACES)
            where[base + target] = (first + batch) * SLOTS + slot


def fetch_lists(lists_in, counts_in, lists, counts, sems):
    copies = (
        pltpu.make_async_copy(lists_in, lists, sems.at[0]),
        pltpu.make_async_copy(counts_in, counts, sems.at[1]),
    )
    for copy in copies:
        copy.start()
    return copies


def fetch_tiles(ratings_in, tiles, visit, batch, sem):
    slots = pl.ds((visit * BATCHES + batch) * SLOTS, SLOTS)
    copy = pltpu.make_async_copy(ratings_in.at[slots], tiles.at[slots], sem)
    copy.start()
    return copy


def first_block_kernel(
    lists_in, counts_in, users_in, items_in, ratings_in,
    users, items_out, blocks_out,
    items, tiles, lists, counts, where, sems,
):
    list_copies = fetch_lists(lists_in, counts_in, lists, counts, sems)
    copies = []

    def pieces(source, target, first, size, count):
        for piece in range(count):
            rows = pl.ds(first + piece * (size // count), size // count)
            copies.append(
                pltpu.make_async_copy(source.at[rows], target.at[rows], sems.at[2 + len(copies)])
            )
            copies[-1].start()

    pieces(items_in, items, 0, ROWS, 1)
    waits = []
    for batch in range(BATCHES):
        pieces(users_in, users, batch * ROWS, ROWS, 1)
        pieces(ratings_in, tiles, batch * SLOTS, SLOTS, 1)
        waits.append(len(copies))
    tiles[LISTED] = jnp.zeros((TILE, TILE), BF16)
    for copy in list_copies:
        copy.wait()
    place_slots(where, lists, counts, 0, 0, LISTED)
    halves = [None] * HALVES
    user_parts = {}

    def users_of(batch):
        if batch not in user_parts:
            user_parts[batch] = split(users[batch_rows(batch)])
        return user_parts[batch]

    def before(kind, half, batch):
        if kind == "P" and half == 0 and batch == 0:
            for copy in copies[: waits[0]]:
                copy.wait()
        if kind == "P" and batch == 0:
            halves[half] = items[half * HALF : (half + 1) * HALF]
        if kind == "P" and half == 0 and batch == 1:
            for copy in copies[waits[0] :]:
                copy.wait()

    block_steps(
        lambda batch, place: tiles[where[batch * (PLACES + 1) + place]],
        users_of,
        halves,
        blocks_out,
        before,
    )
    store_coded(halves, items_out)


def first_users_kernel(
    lists_in, counts_in, ratings_in, users, blocks,
    users_out, parts_out, later_out,
    tiles, lists, counts, where, sems,
):
    list_copies = fetch_lists(lists_in, counts_in, lists, counts, sems)
    tile_copies = [
        fetch_tiles(ratings_in, tiles, visit, batch, sems.at[2 + visit * BATCHES + batch])
        for visit in range(VISITS)
        for batch in range(BATCHES)
    ]
    tiles[NONE] = jnp.zeros((TILE, TILE), BF16)
    for copy in list_copies + tuple(tile_copies):
        copy.wait()
    for visit in range(VISITS):
        place_slots(where, lists, counts, visit, visit * BATCHES, NONE)
    for batch in range(BATCHES):
        rows = batch_rows(batch)
        old = users[rows]
        new = users_step(
            old,
            split(old),
            (blocks[batch, 0], blocks[batch, 1]),
            lambda place: tiles[where[batch * (PLACES + 1) + place]],
        )
        users_out[rows] = new
        parts_out[0, rows], parts_out[1, rows] = split(new)
    for batch in range(BATCHES):
        for place in range(PLACES):
            slot = where[(BATCHES + batch) * (PLACES + 1) + place]
            later_out[batch * PLACES + place] = tiles[slot]


def second_block_kernel(parts, items_in, later, items_out, blocks_out):
    halves = [decode(items_in, half) for half in range(HALVES)]
    block_steps(
        lambda batch, place: later[batch * PLACES + place],
        lambda batch: (parts[0, batch_rows(batch)], parts[1, batch_rows(batch)]),
        halves,
        blocks_out,
    )
    store_coded(halves, items_out)


def second_users_kernel(users, parts, blocks, later, users_out, fresh, sems):
    copies = []
    for batch in range(BATCHES):
        rows = batch_rows(batch)
        fresh[rows] = users_step(
            users[rows],
            (parts[0, rows], parts[1, rows]),
            (blocks[batch, 0], blocks[batch, 1]),
            lambda place: later[batch * PLACES + place],
        )
        copies.append(
            pltpu.make_async_copy(fresh.at[rows], users_out.at[rows], sems.at[batch])
        )
        copies[-1].start()
    for copy in copies:
        copy.wait()


def held(value):
    return pltpu.with_memory_space_constraint(value, pltpu.HBM)


SPEC_HBM = pl.BlockSpec(memory_space=pltpu.HBM)
SPEC_VMEM = pl.BlockSpec(memory_space=pltpu.VMEM)
CODED_SHAPE = jax.ShapeDtypeStruct((ROWS + EXTRA, RANK), jnp.int16)
USERS_SHAPE = jax.ShapeDtypeStruct((BATCHES * ROWS, RANK), F32)
PARTS_SHAPE = jax.ShapeDtypeStruct((2, BATCHES * ROWS, RANK), BF16)
LATER_SHAPE = jax.ShapeDtypeStruct((BATCHES * PLACES, TILE, TILE), BF16)
BLOCKS_SHAPE = jax.ShapeDtypeStruct((BATCHES, 2, ROWS, RANK), BF16)
PRODUCT_FLOPS = 2 * 3 * BATCHES * ROWS * ROWS * RANK


def call(kernel, name, outs, out_specs, in_specs, scratch, products, args):
    return pl.pallas_call(
        kernel,
        out_shape=outs,
        in_specs=in_specs,
        out_specs=out_specs,
        scratch_shapes=scratch,
        compiler_params=pltpu.CompilerParams(vmem_limit_bytes=28 * 1024 * 1024),
        cost_estimate=pl.CostEstimate(
            flops=products * PRODUCT_FLOPS, bytes_accessed=1 << 20, transcendentals=0
        ),
        name=name,
    )(*args)


def list_scratch(visits):
    return [
        pltpu.VMEM((visits * LISTED + 1, TILE, TILE), BF16),
        pltpu.SMEM((ENTRIES, 2, SLOTS), jnp.int32),
        pltpu.SMEM((ENTRIES,), jnp.int32),
        pltpu.SMEM((visits * BATCHES * (PLACES + 1),), jnp.int32),
    ]


def first_block(lists, counts, users, items, ratings):
    return call(
        first_block_kernel,
        "first_block",
        (USERS_SHAPE, CODED_SHAPE, BLOCKS_SHAPE),
        (SPEC_VMEM,) * 3,
        [SPEC_HBM] * 5,
        [pltpu.VMEM((ROWS, RANK), F32), *list_scratch(1), pltpu.SemaphoreType.DMA((7,))],
        2,
        (held(lists), held(counts), held(users), held(items), held(ratings)),
    )


def first_users(lists, counts, ratings, users, blocks):
    return call(
        first_users_kernel,
        "first_users",
        (USERS_SHAPE, PARTS_SHAPE, LATER_SHAPE),
        (SPEC_VMEM,) * 3,
        [SPEC_HBM] * 3 + [SPEC_VMEM] * 2,
        [*list_scratch(VISITS), pltpu.SemaphoreType.DMA((2 + ENTRIES,))],
        2,
        (held(lists), held(counts), held(ratings), users, blocks),
    )


def second_block(parts, items, later):
    return call(
        second_block_kernel,
        "second_block",
        (CODED_SHAPE, BLOCKS_SHAPE),
        (SPEC_VMEM,) * 2,
        [SPEC_VMEM] * 3,
        [],
        2,
        (parts, items, later),
    )


def second_users(users, parts, blocks, later):
    return call(
        second_users_kernel,
        "second_users",
        USERS_SHAPE,
        SPEC_HBM,
        [SPEC_VMEM] * 4,
        [pltpu.VMEM((BATCHES * ROWS, RANK), F32), pltpu.SemaphoreType.DMA((BATCHES,))],
        2,
        (users, parts, blocks, later),
    )


PIECE = 128


def unpack_kernel(coded, items_out, items, sems):
    copies = []
    for piece in range(ROWS // PIECE):
        half, first = divmod(piece * PIECE, HALF)
        rows = pl.ds(piece * PIECE, PIECE)
        items[rows] = decode(coded, half, first, PIECE)
        copies.append(pltpu.make_async_copy(items.at[rows], items_out.at[rows], sems.at[piece]))
        copies[-1].start()
    for copy in copies:
        copy.wait()


def unpack(coded):
    return pl.pallas_call(
        unpack_kernel,
        out_shape=jax.ShapeDtypeStruct((ROWS, RANK), F32),
        in_specs=[SPEC_VMEM],
        out_specs=SPEC_HBM,
        scratch_shapes=[
            pltpu.VMEM((ROWS, RANK), F32),
            pltpu.SemaphoreType.DMA((ROWS // PIECE,)),
        ],
        compiler_params=pltpu.CompilerParams(vmem_limit_bytes=8 * 1024 * 1024),
        name="unpack",
    )(coded)


def on_device(user_factors, item_factors, ratings, tile_lists, tile_counts):
    users, coded, blocks = first_block(
        tile_lists, tile_counts, user_factors, item_factors, ratings
    )
    arrived = passed_along(coded, "blk", 1)
    users, parts, later = first_users(tile_lists, tile_counts, ratings, users, blocks)
    coded, blocks = second_block(parts, arrived, later)
    returned = passed_along(coded, "blk", -1)
    users = second_users(users, parts, blocks, later)
    items = unpack(returned)
    return (users, items)


def solution(mesh):
    in_specs = (
        P(("grp", "blk"), None),
        P(("grp", "blk"), None),
        P(("grp", "blk"), None, None),
        P(("grp", "blk"), None, None),
        P(("grp", "blk")),
    )
    out_specs = (P(("grp", "blk"), None), P(("grp", "blk"), None))
    return jax.shard_map(
        on_device, mesh=mesh, in_specs=in_specs, out_specs=out_specs, check_vma=False
    )
```

time: 38.9 us -> 38.2 us (0.982)
  waiting for transfers between devices: 19.2 us -> 14.9 us
  Pallas kernels: 10.9 us -> 14.5 us
    ppermute x2, waiting for transfers between devices: 19.2 us -> 14.9 us  [passed_along(): return lax.ppermute(value, axis, pairs)]
    pallas_call x4, Pallas kernels: 10.1 us -> 13.7 us  [call(): pl.pallas_call(kernel, out_shape=outs, in_specs=in_specs, out_specs=out_s...]
  transfers between devices with their start and end apart: 2 -> 2, of which waited for: 2 -> 2; matrix products, arithmetic and copies ran while one was open for 0% -> 0% of each run, Pallas kernels for 9% -> 19%
where the time goes in v4:
time: 38.2 us; the launch traced here: 38 us
  waiting for transfers between devices  14.9 us (39%)
  Pallas kernels  14.5 us (38%)
  starting transfers between devices  7.91 us (21%)
  between operations  0.68 us (2%)
    ppermute x2, waiting for transfers between devices, passed_along(): return lax.ppermute(value, axis, pairs)  14.9 us
    pallas_call x4, Pallas kernels, call(): pl.pallas_call(kernel, out_shape=outs, in_specs=in_specs, out_specs=out_s...  13.7 us
    ppermute x2, starting transfers between devices, passed_along(): return lax.ppermute(value, axis, pairs)  7.91 us
    pallas_call x1, Pallas kernels, unpack(): pl.pallas_call(unpack_kernel, out_shape=jax.ShapeDtypeStruct((ROWS, RANK)...  0.84 us
  transfers between devices with their start and end apart: 2, of which 2 were waited for; matrix products, arithmetic and copies ran while one was open for 0% of the time, Pallas kernels for 19%

profile of v4, /device:TPU:16, one launch (start us, length us, event | category | flops | bytes accessed | tf_op | source)
XLA Modules:
  0.0 38.0 jit_solution(746218020154845863)
XLA Ops:
  0.6 3.9 %first_block.1 = (f32[1024,256]{1,0:T(8,128)S(1)}, s16[528,256]{1,0:T(8,128)(2,1)S(1)}, bf16[2,2,512,256]{3,2,1,0:T(8,128)(2,1)S(1)}) custom-call(s32[4,2,12]{2,1,0:T(2,128)} %lists_in.3, s32[4]{0:T(128)} %counts_in.3, f32[1024,256]{1,0:T(8,128)} %users_in.1, f32[512,256]{1,0:T(8,128)} %items_in.1, bf16[48,128,128]{2,1,0:T(8,128)(2,1)} %ratings_in.3), custom_call_target="tpu_custom_call" | custom-call | flops 1610612736 | bytes 1048576 | tf_op jit(solution)/shard_map/first_block/pallas_call | solution.py:298
  4.5 4.3 %collective-permute-start = (s16[528,256]{1,0:T(8,128)(2,1)S(1)}, s16[528,256]{1,0:T(8,128)(2,1)S(1)}, u32[]{:S(2)}, u32[]{:S(2)}) collective-permute-start(s16[528,256]{1,0:T(8,128)(2,1)S(1)} %get-tuple-element.14), channel_id=1, source_target_pairs={{0,8},{8,16},{16,24},{24,32},{32,40},{40,48},{48,56},{56,64},{64,7... | collective-permute-start | bytes 811016 | tf_op jit(solution)/shard_map/ppermute | solution.py:33
  8.8 4.0 %first_users.1 = (f32[1024,256]{1,0:T(8,128)S(1)}, bf16[2,1024,256]{2,1,0:T(8,128)(2,1)S(1)}, bf16[32,128,128]{2,1,0:T(8,128)(2,1)S(1)}) custom-call(s32[4,2,12]{2,1,0:T(2,128)} %lists_in.3, s32[4]{0:T(128)} %counts_in.3, bf16[48,128,128]{2,1,0:T(8,128)(2,1)} %ratings_in.3, f32[1024,256]{1,0:T(8,128)S(1)} %get-tuple-element.10.users, ...), custom_call_target="tpu_custom_call" | custom-call | flops 1610612736 | bytes 1048576 | tf_op jit(solution)/shard_map/first_users/pallas_call | solution.py:298
  12.8 12.4 %collective-permute-done.items_in = s16[528,256]{1,0:T(8,128)(2,1)S(1)} collective-permute-done((s16[528,256]{1,0:T(8,128)(2,1)S(1)}, s16[528,256]{1,0:T(8,128)(2,1)S(1)}, u32[]{:S(2)}, u32[]{:S(2)}) %collective-permute-start) | collective-permute-done | bytes 270368 | tf_op jit(solution)/shard_map/ppermute | solution.py:33
  25.2 2.5 %second_block.1 = (s16[528,256]{1,0:T(8,128)(2,1)S(1)}, bf16[2,2,512,256]{3,2,1,0:T(8,128)(2,1)S(1)}) custom-call(bf16[2,1024,256]{2,1,0:T(8,128)(2,1)S(1)} %get-tuple-element.13.parts, s16[528,256]{1,0:T(8,128)(2,1)S(1)} %collective-permute-done.items_in, bf16[32,128,128]{2,1,0:T(8,128)(2,1)S(1)} %get-tuple-element.15.later), custom_call_target="tpu_custom_call" | custom-call | flops 1610612736 | bytes 1048576 | tf_op jit(solution)/shard_map/second_block/pallas_call | solution.py:298
  27.6 3.6 %collective-permute-start.1 = (s16[528,256]{1,0:T(8,128)(2,1)S(1)}, s16[528,256]{1,0:T(8,128)(2,1)S(1)}, u32[]{:S(2)}, u32[]{:S(2)}) collective-permute-start(s16[528,256]{1,0:T(8,128)(2,1)S(1)} %get-tuple-element.17), channel_id=1, source_target_pairs={{0,504},{8,0},{16,8},{24,16},{32,24},{40,32},{48,40},{56,48},{64,5... | collective-permute-start | bytes 811016 | tf_op jit(solution)/shard_map/ppermute | solution.py:33
  31.3 3.4 %second_users.1 = f32[1024,256]{1,0:T(8,128)} custom-call(f32[1024,256]{1,0:T(8,128)S(1)} %get-tuple-element.12.users, bf16[2,1024,256]{2,1,0:T(8,128)(2,1)S(1)} %get-tuple-element.13.parts, bf16[2,2,512,256]{3,2,1,0:T(8,128)(2,1)S(1)} %get-tuple-element.16.blocks, bf16[32,128,128]{2,1,0:T(8,128)(2,1)S(1)} %get-tuple-element.15.later), custom_call_target="tpu_custom_call" | custom-call | flops 1610612736 | bytes 1048576 | tf_op jit(solution)/shard_map/second_users/pallas_call | solution.py:298
  34.6 2.6 %collective-permute-done.1.coded = s16[528,256]{1,0:T(8,128)(2,1)S(1)} collective-permute-done((s16[528,256]{1,0:T(8,128)(2,1)S(1)}, s16[528,256]{1,0:T(8,128)(2,1)S(1)}, u32[]{:S(2)}, u32[]{:S(2)}) %collective-permute-start.1) | collective-permute-done | bytes 270368 | tf_op jit(solution)/shard_map/ppermute | solution.py:33
  37.2 0.8 %unpack.1 = f32[512,256]{1,0:T(8,128)} custom-call(s16[528,256]{1,0:T(8,128)(2,1)S(1)} %collective-permute-done.1.coded), custom_call_target="tpu_custom_call" | custom-call | tf_op jit(solution)/shard_map/unpack/pallas_call | solution.py:389
Async XLA Ops:
  4.5 20.6 %collective-permute-start = (s16[528,256]{1,0:T(8,128)(2,1)S(1)}, s16[528,256]{1,0:T(8,128)(2,1)S(1)}, u32[]{:S(2)}, u32[]{:S(2)}) collective-permute-start(s16[528,256]{1,0:T(8,128)(2,1)S(1)} %get-tuple-element.14), channel_id=1, source_target_pairs={{0,8},{8,16},{16,24},{24,32},{32,40},{40,48},{48,56},{56,64},{64,7... | collective-permute-start | bytes 811016 | tf_op jit(solution)/shard_map/ppermute | solution.py:33
  27.6 9.6 %collective-permute-start.1 = (s16[528,256]{1,0:T(8,128)(2,1)S(1)}, s16[528,256]{1,0:T(8,128)(2,1)S(1)}, u32[]{:S(2)}, u32[]{:S(2)}) collective-permute-start(s16[528,256]{1,0:T(8,128)(2,1)S(1)} %get-tuple-element.17), channel_id=1, source_target_pairs={{0,504},{8,0},{16,8},{24,16},{32,24},{40,32},{48,40},{56,48},{64,5... | collective-permute-start | bytes 811016 | tf_op jit(solution)/shard_map/ppermute | solution.py:33

commit v5 on v4

--- a/solution.py
+++ b/solution.py
@@ -86,14 +86,15 @@
     return jnp.concatenate(highs, axis=0), jnp.concatenate(lows, axis=0)
 
 
-ORDER = "P00 P10 R00 R10 G00 G10 P01 P11 R01 R11 G01 G11"
+ORDER = tuple(
+    (kind, half, batch) for batch in range(BATCHES) for kind in "PRG" for half in range(HALVES)
+)
 
 
 def block_steps(observed_tile, users_of, halves, blocks_out, before=None):
     parts, predicted, residues = {}, {}, {}
     columns = SIDE // HALVES
-    for item in ORDER.split():
-        kind, half, batch = item[0], int(item[1]), int(item[2])
+    for kind, half, batch in ORDER:
         span = pl.ds(half * HALF, HALF)
         if before is not None:
             before(kind, half, batch)

time: 38.2 us -> 38.2 us (level)
  no operation moved by 1% of the time
where the time goes in v5:
time: 38.2 us; the launch traced here: 38 us
  waiting for transfers between devices  14.9 us (39%)
  Pallas kernels  14.5 us (38%)
  starting transfers between devices  7.91 us (21%)
  between operations  0.68 us (2%)
    ppermute x2, waiting for transfers between devices, passed_along(): return lax.ppermute(value, axis, pairs)  14.9 us
    pallas_call x4, Pallas kernels, call(): pl.pallas_call(kernel, out_shape=outs, in_specs=in_specs, out_specs=out_s...  13.7 us
    ppermute x2, starting transfers between devices, passed_along(): return lax.ppermute(value, axis, pairs)  7.91 us
    pallas_call x1, Pallas kernels, unpack(): pl.pallas_call(unpack_kernel, out_shape=jax.ShapeDtypeStruct((ROWS, RANK)...  0.84 us
  transfers between devices with their start and end apart: 2, of which 2 were waited for; matrix products, arithmetic and copies ran while one was open for 0% of the time, Pallas kernels for 19%

profile of v5, /device:TPU:16, one launch (start us, length us, event | category | flops | bytes accessed | tf_op | source)
XLA Modules:
  0.0 38.0 jit_solution(746218020154845863)
XLA Ops:
  0.6 3.9 %first_block.1 = (f32[1024,256]{1,0:T(8,128)S(1)}, s16[528,256]{1,0:T(8,128)(2,1)S(1)}, bf16[2,2,512,256]{3,2,1,0:T(8,128)(2,1)S(1)}) custom-call(s32[4,2,12]{2,1,0:T(2,128)} %lists_in.3, s32[4]{0:T(128)} %counts_in.3, f32[1024,256]{1,0:T(8,128)} %users_in.1, f32[512,256]{1,0:T(8,128)} %items_in.1, bf16[48,128,128]{2,1,0:T(8,128)(2,1)} %ratings_in.3), custom_call_target="tpu_custom_call" | custom-call | flops 1610612736 | bytes 1048576 | tf_op jit(solution)/shard_map/first_block/pallas_call | solution.py:299
  4.5 4.3 %collective-permute-start = (s16[528,256]{1,0:T(8,128)(2,1)S(1)}, s16[528,256]{1,0:T(8,128)(2,1)S(1)}, u32[]{:S(2)}, u32[]{:S(2)}) collective-permute-start(s16[528,256]{1,0:T(8,128)(2,1)S(1)} %get-tuple-element.14), channel_id=1, source_target_pairs={{0,8},{8,16},{16,24},{24,32},{32,40},{40,48},{48,56},{56,64},{64,7... | collective-permute-start | bytes 811016 | tf_op jit(solution)/shard_map/ppermute | solution.py:33
  8.8 4.0 %first_users.1 = (f32[1024,256]{1,0:T(8,128)S(1)}, bf16[2,1024,256]{2,1,0:T(8,128)(2,1)S(1)}, bf16[32,128,128]{2,1,0:T(8,128)(2,1)S(1)}) custom-call(s32[4,2,12]{2,1,0:T(2,128)} %lists_in.3, s32[4]{0:T(128)} %counts_in.3, bf16[48,128,128]{2,1,0:T(8,128)(2,1)} %ratings_in.3, f32[1024,256]{1,0:T(8,128)S(1)} %get-tuple-element.10.users, ...), custom_call_target="tpu_custom_call" | custom-call | flops 1610612736 | bytes 1048576 | tf_op jit(solution)/shard_map/first_users/pallas_call | solution.py:299
  12.8 12.4 %collective-permute-done.items_in = s16[528,256]{1,0:T(8,128)(2,1)S(1)} collective-permute-done((s16[528,256]{1,0:T(8,128)(2,1)S(1)}, s16[528,256]{1,0:T(8,128)(2,1)S(1)}, u32[]{:S(2)}, u32[]{:S(2)}) %collective-permute-start) | collective-permute-done | bytes 270368 | tf_op jit(solution)/shard_map/ppermute | solution.py:33
  25.2 2.5 %second_block.1 = (s16[528,256]{1,0:T(8,128)(2,1)S(1)}, bf16[2,2,512,256]{3,2,1,0:T(8,128)(2,1)S(1)}) custom-call(bf16[2,1024,256]{2,1,0:T(8,128)(2,1)S(1)} %get-tuple-element.13.parts, s16[528,256]{1,0:T(8,128)(2,1)S(1)} %collective-permute-done.items_in, bf16[32,128,128]{2,1,0:T(8,128)(2,1)S(1)} %get-tuple-element.15.later), custom_call_target="tpu_custom_call" | custom-call | flops 1610612736 | bytes 1048576 | tf_op jit(solution)/shard_map/second_block/pallas_call | solution.py:299
  27.6 3.6 %collective-permute-start.1 = (s16[528,256]{1,0:T(8,128)(2,1)S(1)}, s16[528,256]{1,0:T(8,128)(2,1)S(1)}, u32[]{:S(2)}, u32[]{:S(2)}) collective-permute-start(s16[528,256]{1,0:T(8,128)(2,1)S(1)} %get-tuple-element.17), channel_id=1, source_target_pairs={{0,504},{8,0},{16,8},{24,16},{32,24},{40,32},{48,40},{56,48},{64,5... | collective-permute-start | bytes 811016 | tf_op jit(solution)/shard_map/ppermute | solution.py:33
  31.3 3.4 %second_users.1 = f32[1024,256]{1,0:T(8,128)} custom-call(f32[1024,256]{1,0:T(8,128)S(1)} %get-tuple-element.12.users, bf16[2,1024,256]{2,1,0:T(8,128)(2,1)S(1)} %get-tuple-element.13.parts, bf16[2,2,512,256]{3,2,1,0:T(8,128)(2,1)S(1)} %get-tuple-element.16.blocks, bf16[32,128,128]{2,1,0:T(8,128)(2,1)S(1)} %get-tuple-element.15.later), custom_call_target="tpu_custom_call" | custom-call | flops 1610612736 | bytes 1048576 | tf_op jit(solution)/shard_map/second_users/pallas_call | solution.py:299
  34.6 2.6 %collective-permute-done.1.coded = s16[528,256]{1,0:T(8,128)(2,1)S(1)} collective-permute-done((s16[528,256]{1,0:T(8,128)(2,1)S(1)}, s16[528,256]{1,0:T(8,128)(2,1)S(1)}, u32[]{:S(2)}, u32[]{:S(2)}) %collective-permute-start.1) | collective-permute-done | bytes 270368 | tf_op jit(solution)/shard_map/ppermute | solution.py:33
  37.2 0.8 %unpack.1 = f32[512,256]{1,0:T(8,128)} custom-call(s16[528,256]{1,0:T(8,128)(2,1)S(1)} %collective-permute-done.1.coded), custom_call_target="tpu_custom_call" | custom-call | tf_op jit(solution)/shard_map/unpack/pallas_call | solution.py:390
Async XLA Ops:
  4.5 20.6 %collective-permute-start = (s16[528,256]{1,0:T(8,128)(2,1)S(1)}, s16[528,256]{1,0:T(8,128)(2,1)S(1)}, u32[]{:S(2)}, u32[]{:S(2)}) collective-permute-start(s16[528,256]{1,0:T(8,128)(2,1)S(1)} %get-tuple-element.14), channel_id=1, source_target_pairs={{0,8},{8,16},{16,24},{24,32},{32,40},{40,48},{48,56},{56,64},{64,7... | collective-permute-start | bytes 811016 | tf_op jit(solution)/shard_map/ppermute | solution.py:33
  27.6 9.6 %collective-permute-start.1 = (s16[528,256]{1,0:T(8,128)(2,1)S(1)}, s16[528,256]{1,0:T(8,128)(2,1)S(1)}, u32[]{:S(2)}, u32[]{:S(2)}) collective-permute-start(s16[528,256]{1,0:T(8,128)(2,1)S(1)} %get-tuple-element.17), channel_id=1, source_target_pairs={{0,504},{8,0},{16,8},{24,16},{32,24},{40,32},{48,40},{56,48},{64,5... | collective-permute-start | bytes 811016 | tf_op jit(solution)/shard_map/ppermute | solution.py:33

commit v6 on v5

--- a/solution.py
+++ b/solution.py
@@ -15,6 +15,7 @@
 RANK = 256
 HALVES = 2
 HALF = ROWS // HALVES
+PIECES = 2
 EXTRA = 16
 ENTRIES = VISITS * BATCHES
 LISTED = BATCHES * SLOTS
@@ -73,7 +74,7 @@
 
 def residue_parts(predicted, observed_tile, columns):
     highs, lows = [], []
-    for row in range(SIDE):
+    for row in range(predicted.shape[0] // TILE):
         high_row, low_row = [], []
         for column in range(columns):
             observed = observed_tile(row, column).astype(F32)
@@ -84,6 +85,11 @@
         highs.append(jnp.concatenate(high_row, axis=1))
         lows.append(jnp.concatenate(low_row, axis=1))
     return jnp.concatenate(highs, axis=0), jnp.concatenate(lows, axis=0)
+
+
+def user_piece(parts, piece):
+    size = ROWS // PIECES
+    return tuple(which[piece * size : (piece + 1) * size] for which in parts)
 
 
 ORDER = tuple(
@@ -102,15 +108,24 @@
             parts[half] = split(halves[half])
             for which in range(2):
                 blocks_out[batch, which, span] = parts[half][which]
-            predicted[half] = product(users_of(batch), parts[half], ((1,), (1,)))
+            predicted[half] = [
+                product(user_piece(users_of(batch), piece), parts[half], ((1,), (1,)))
+                for piece in range(PIECES)
+            ]
         elif kind == "R":
-            residues[half] = residue_parts(
-                predicted[half],
-                lambda row, column: observed_tile(batch, row * SIDE + half * columns + column),
-                columns,
-            )
+            residues[half] = [
+                residue_parts(
+                    predicted[half][piece],
+                    lambda row, column: observed_tile(
+                        batch, (row + piece * (SIDE // PIECES)) * SIDE + half * columns + column
+                    ),
+                    columns,
+                )
+                for piece in range(PIECES)
+            ]
         else:
-            grad_items = product(residues[half], users_of(batch), ((0,), (0,)))
+            whole = tuple(jnp.concatenate(which, axis=0) for which in zip(*residues[half]))
+            grad_items = product(whole, users_of(batch), ((0,), (0,)))
             halves[half] = halves[half] - LEARN * (grad_items + DECAY * halves[half])
 
 
@@ -201,10 +216,12 @@
 
     def before(kind, half, batch):
         if kind == "P" and half == 0 and batch == 0:
-            for copy in copies[: waits[0]]:
+            for copy in copies[: waits[0] - 1]:
                 copy.wait()
         if kind == "P" and batch == 0:
             halves[half] = items[half * HALF : (half + 1) * HALF]
+        if kind == "R" and half == 0 and batch == 0:
+            copies[waits[0] - 1].wait()
         if kind == "P" and half == 0 and batch == 1:
             for copy in copies[waits[0] :]:
                 copy.wait()

time: 38.2 us -> 38 us (level)
  no operation moved by 1% of the time
where the time goes in v6:
time: 38 us; the launch traced here: 37.8 us
  waiting for transfers between devices  14.9 us (39%)
  Pallas kernels  14.3 us (38%)
  starting transfers between devices  7.94 us (21%)
  between operations  0.68 us (2%)
    ppermute x2, waiting for transfers between devices, passed_along(): return lax.ppermute(value, axis, pairs)  14.9 us
    pallas_call x4, Pallas kernels, call(): pl.pallas_call(kernel, out_shape=outs, in_specs=in_specs, out_specs=out_s...  13.5 us
    ppermute x2, starting transfers between devices, passed_along(): return lax.ppermute(value, axis, pairs)  7.94 us
    pallas_call x1, Pallas kernels, unpack(): pl.pallas_call(unpack_kernel, out_shape=jax.ShapeDtypeStruct((ROWS, RANK)...  0.84 us
  transfers between devices with their start and end apart: 2, of which 2 were waited for; matrix products, arithmetic and copies ran while one was open for 0% of the time, Pallas kernels for 19%

profile of v6, /device:TPU:16, one launch (start us, length us, event | category | flops | bytes accessed | tf_op | source)
XLA Modules:
  0.0 37.8 jit_solution(6431244118972643528)
XLA Ops:
  0.6 3.9 %first_block.1 = (f32[1024,256]{1,0:T(8,128)S(1)}, s16[528,256]{1,0:T(8,128)(2,1)S(1)}, bf16[2,2,512,256]{3,2,1,0:T(8,128)(2,1)S(1)}) custom-call(s32[4,2,12]{2,1,0:T(2,128)} %lists_in.3, s32[4]{0:T(128)} %counts_in.3, f32[1024,256]{1,0:T(8,128)} %users_in.1, f32[512,256]{1,0:T(8,128)} %items_in.1, bf16[48,128,128]{2,1,0:T(8,128)(2,1)} %ratings_in.3), custom_call_target="tpu_custom_call" | custom-call | flops 1610612736 | bytes 1048576 | tf_op jit(solution)/shard_map/first_block/pallas_call | solution.py:316
  4.5 4.3 %collective-permute-start = (s16[528,256]{1,0:T(8,128)(2,1)S(1)}, s16[528,256]{1,0:T(8,128)(2,1)S(1)}, u32[]{:S(2)}, u32[]{:S(2)}) collective-permute-start(s16[528,256]{1,0:T(8,128)(2,1)S(1)} %get-tuple-element.14), channel_id=1, source_target_pairs={{0,8},{8,16},{16,24},{24,32},{32,40},{40,48},{48,56},{56,64},{64,7... | collective-permute-start | bytes 811016 | tf_op jit(solution)/shard_map/ppermute | solution.py:34
  8.8 4.0 %first_users.1 = (f32[1024,256]{1,0:T(8,128)S(1)}, bf16[2,1024,256]{2,1,0:T(8,128)(2,1)S(1)}, bf16[32,128,128]{2,1,0:T(8,128)(2,1)S(1)}) custom-call(s32[4,2,12]{2,1,0:T(2,128)} %lists_in.3, s32[4]{0:T(128)} %counts_in.3, bf16[48,128,128]{2,1,0:T(8,128)(2,1)} %ratings_in.3, f32[1024,256]{1,0:T(8,128)S(1)} %get-tuple-element.10.users, ...), custom_call_target="tpu_custom_call" | custom-call | flops 1610612736 | bytes 1048576 | tf_op jit(solution)/shard_map/first_users/pallas_call | solution.py:316
  12.8 12.4 %collective-permute-done.items_in = s16[528,256]{1,0:T(8,128)(2,1)S(1)} collective-permute-done((s16[528,256]{1,0:T(8,128)(2,1)S(1)}, s16[528,256]{1,0:T(8,128)(2,1)S(1)}, u32[]{:S(2)}, u32[]{:S(2)}) %collective-permute-start) | collective-permute-done | bytes 270368 | tf_op jit(solution)/shard_map/ppermute | solution.py:34
  25.1 2.3 %second_block.1 = (s16[528,256]{1,0:T(8,128)(2,1)S(1)}, bf16[2,2,512,256]{3,2,1,0:T(8,128)(2,1)S(1)}) custom-call(bf16[2,1024,256]{2,1,0:T(8,128)(2,1)S(1)} %get-tuple-element.13.parts, s16[528,256]{1,0:T(8,128)(2,1)S(1)} %collective-permute-done.items_in, bf16[32,128,128]{2,1,0:T(8,128)(2,1)S(1)} %get-tuple-element.15.later), custom_call_target="tpu_custom_call" | custom-call | flops 1610612736 | bytes 1048576 | tf_op jit(solution)/shard_map/second_block/pallas_call | solution.py:316
  27.4 3.7 %collective-permute-start.1 = (s16[528,256]{1,0:T(8,128)(2,1)S(1)}, s16[528,256]{1,0:T(8,128)(2,1)S(1)}, u32[]{:S(2)}, u32[]{:S(2)}) collective-permute-start(s16[528,256]{1,0:T(8,128)(2,1)S(1)} %get-tuple-element.17), channel_id=1, source_target_pairs={{0,504},{8,0},{16,8},{24,16},{32,24},{40,32},{48,40},{56,48},{64,5... | collective-permute-start | bytes 811016 | tf_op jit(solution)/shard_map/ppermute | solution.py:34
  31.1 3.4 %second_users.1 = f32[1024,256]{1,0:T(8,128)} custom-call(f32[1024,256]{1,0:T(8,128)S(1)} %get-tuple-element.12.users, bf16[2,1024,256]{2,1,0:T(8,128)(2,1)S(1)} %get-tuple-element.13.parts, bf16[2,2,512,256]{3,2,1,0:T(8,128)(2,1)S(1)} %get-tuple-element.16.blocks, bf16[32,128,128]{2,1,0:T(8,128)(2,1)S(1)} %get-tuple-element.15.later), custom_call_target="tpu_custom_call" | custom-call | flops 1610612736 | bytes 1048576 | tf_op jit(solution)/shard_map/second_users/pallas_call | solution.py:316
  34.5 2.5 %collective-permute-done.1.coded = s16[528,256]{1,0:T(8,128)(2,1)S(1)} collective-permute-done((s16[528,256]{1,0:T(8,128)(2,1)S(1)}, s16[528,256]{1,0:T(8,128)(2,1)S(1)}, u32[]{:S(2)}, u32[]{:S(2)}) %collective-permute-start.1) | collective-permute-done | bytes 270368 | tf_op jit(solution)/shard_map/ppermute | solution.py:34
  37.0 0.8 %unpack.1 = f32[512,256]{1,0:T(8,128)} custom-call(s16[528,256]{1,0:T(8,128)(2,1)S(1)} %collective-permute-done.1.coded), custom_call_target="tpu_custom_call" | custom-call | tf_op jit(solution)/shard_map/unpack/pallas_call | solution.py:407
Async XLA Ops:
  4.5 20.6 %collective-permute-start = (s16[528,256]{1,0:T(8,128)(2,1)S(1)}, s16[528,256]{1,0:T(8,128)(2,1)S(1)}, u32[]{:S(2)}, u32[]{:S(2)}) collective-permute-start(s16[528,256]{1,0:T(8,128)(2,1)S(1)} %get-tuple-element.14), channel_id=1, source_target_pairs={{0,8},{8,16},{16,24},{24,32},{32,40},{40,48},{48,56},{56,64},{64,7... | collective-permute-start | bytes 811016 | tf_op jit(solution)/shard_map/ppermute | solution.py:34
  27.4 9.6 %collective-permute-start.1 = (s16[528,256]{1,0:T(8,128)(2,1)S(1)}, s16[528,256]{1,0:T(8,128)(2,1)S(1)}, u32[]{:S(2)}, u32[]{:S(2)}) collective-permute-start(s16[528,256]{1,0:T(8,128)(2,1)S(1)} %get-tuple-element.17), channel_id=1, source_target_pairs={{0,504},{8,0},{16,8},{24,16},{32,24},{40,32},{48,40},{56,48},{64,5... | collective-permute-start | bytes 811016 | tf_op jit(solution)/shard_map/ppermute | solution.py:34

commit v7 on v6

--- a/solution.py
+++ b/solution.py
@@ -221,9 +221,7 @@
         if kind == "P" and batch == 0:
             halves[half] = items[half * HALF : (half + 1) * HALF]
         if kind == "R" and half == 0 and batch == 0:
-            copies[waits[0] - 1].wait()
-        if kind == "P" and half == 0 and batch == 1:
-            for copy in copies[waits[0] :]:
+            for copy in copies[waits[0] - 1 :]:
                 copy.wait()
 
     block_steps(

time: 38 us -> 37.9 us (level)
  no operation moved by 1% of the time
where the time goes in v7:
time: 37.9 us; the launch traced here: 37.7 us
  waiting for transfers between devices  14.9 us (39%)
  Pallas kernels  14.2 us (37%)
  starting transfers between devices  7.92 us (21%)
  between operations  0.68 us (2%)
    ppermute x2, waiting for transfers between devices, passed_along(): return lax.ppermute(value, axis, pairs)  14.9 us
    pallas_call x4, Pallas kernels, call(): pl.pallas_call(kernel, out_shape=outs, in_specs=in_specs, out_specs=out_s...  13.4 us
    ppermute x2, starting transfers between devices, passed_along(): return lax.ppermute(value, axis, pairs)  7.92 us
    pallas_call x1, Pallas kernels, unpack(): pl.pallas_call(unpack_kernel, out_shape=jax.ShapeDtypeStruct((ROWS, RANK)...  0.84 us
  transfers between devices with their start and end apart: 2, of which 2 were waited for; matrix products, arithmetic and copies ran while one was open for 0% of the time, Pallas kernels for 19%

profile of v7, /device:TPU:16, one launch (start us, length us, event | category | flops | bytes accessed | tf_op | source)
XLA Modules:
  0.0 37.7 jit_solution(5893346557502339833)
XLA Ops:
  0.6 3.8 %first_block.1 = (f32[1024,256]{1,0:T(8,128)S(1)}, s16[528,256]{1,0:T(8,128)(2,1)S(1)}, bf16[2,2,512,256]{3,2,1,0:T(8,128)(2,1)S(1)}) custom-call(s32[4,2,12]{2,1,0:T(2,128)} %lists_in.3, s32[4]{0:T(128)} %counts_in.3, f32[1024,256]{1,0:T(8,128)} %users_in.1, f32[512,256]{1,0:T(8,128)} %items_in.1, bf16[48,128,128]{2,1,0:T(8,128)(2,1)} %ratings_in.3), custom_call_target="tpu_custom_call" | custom-call | flops 1610612736 | bytes 1048576 | tf_op jit(solution)/shard_map/first_block/pallas_call | solution.py:314
  4.4 4.3 %collective-permute-start = (s16[528,256]{1,0:T(8,128)(2,1)S(1)}, s16[528,256]{1,0:T(8,128)(2,1)S(1)}, u32[]{:S(2)}, u32[]{:S(2)}) collective-permute-start(s16[528,256]{1,0:T(8,128)(2,1)S(1)} %get-tuple-element.14), channel_id=1, source_target_pairs={{0,8},{8,16},{16,24},{24,32},{32,40},{40,48},{48,56},{56,64},{64,7... | collective-permute-start | bytes 811016 | tf_op jit(solution)/shard_map/ppermute | solution.py:34
  8.7 4.0 %first_users.1 = (f32[1024,256]{1,0:T(8,128)S(1)}, bf16[2,1024,256]{2,1,0:T(8,128)(2,1)S(1)}, bf16[32,128,128]{2,1,0:T(8,128)(2,1)S(1)}) custom-call(s32[4,2,12]{2,1,0:T(2,128)} %lists_in.3, s32[4]{0:T(128)} %counts_in.3, bf16[48,128,128]{2,1,0:T(8,128)(2,1)} %ratings_in.3, f32[1024,256]{1,0:T(8,128)S(1)} %get-tuple-element.10.users, ...), custom_call_target="tpu_custom_call" | custom-call | flops 1610612736 | bytes 1048576 | tf_op jit(solution)/shard_map/first_users/pallas_call | solution.py:314
  12.7 12.4 %collective-permute-done.items_in = s16[528,256]{1,0:T(8,128)(2,1)S(1)} collective-permute-done((s16[528,256]{1,0:T(8,128)(2,1)S(1)}, s16[528,256]{1,0:T(8,128)(2,1)S(1)}, u32[]{:S(2)}, u32[]{:S(2)}) %collective-permute-start) | collective-permute-done | bytes 270368 | tf_op jit(solution)/shard_map/ppermute | solution.py:34
  25.0 2.3 %second_block.1 = (s16[528,256]{1,0:T(8,128)(2,1)S(1)}, bf16[2,2,512,256]{3,2,1,0:T(8,128)(2,1)S(1)}) custom-call(bf16[2,1024,256]{2,1,0:T(8,128)(2,1)S(1)} %get-tuple-element.13.parts, s16[528,256]{1,0:T(8,128)(2,1)S(1)} %collective-permute-done.items_in, bf16[32,128,128]{2,1,0:T(8,128)(2,1)S(1)} %get-tuple-element.15.later), custom_call_target="tpu_custom_call" | custom-call | flops 1610612736 | bytes 1048576 | tf_op jit(solution)/shard_map/second_block/pallas_call | solution.py:314
  27.3 3.6 %collective-permute-start.1 = (s16[528,256]{1,0:T(8,128)(2,1)S(1)}, s16[528,256]{1,0:T(8,128)(2,1)S(1)}, u32[]{:S(2)}, u32[]{:S(2)}) collective-permute-start(s16[528,256]{1,0:T(8,128)(2,1)S(1)} %get-tuple-element.17), channel_id=1, source_target_pairs={{0,504},{8,0},{16,8},{24,16},{32,24},{40,32},{48,40},{56,48},{64,5... | collective-permute-start | bytes 811016 | tf_op jit(solution)/shard_map/ppermute | solution.py:34
  31.0 3.4 %second_users.1 = f32[1024,256]{1,0:T(8,128)} custom-call(f32[1024,256]{1,0:T(8,128)S(1)} %get-tuple-element.12.users, bf16[2,1024,256]{2,1,0:T(8,128)(2,1)S(1)} %get-tuple-element.13.parts, bf16[2,2,512,256]{3,2,1,0:T(8,128)(2,1)S(1)} %get-tuple-element.16.blocks, bf16[32,128,128]{2,1,0:T(8,128)(2,1)S(1)} %get-tuple-element.15.later), custom_call_target="tpu_custom_call" | custom-call | flops 1610612736 | bytes 1048576 | tf_op jit(solution)/shard_map/second_users/pallas_call | solution.py:314
  34.3 2.5 %collective-permute-done.1.coded = s16[528,256]{1,0:T(8,128)(2,1)S(1)} collective-permute-done((s16[528,256]{1,0:T(8,128)(2,1)S(1)}, s16[528,256]{1,0:T(8,128)(2,1)S(1)}, u32[]{:S(2)}, u32[]{:S(2)}) %collective-permute-start.1) | collective-permute-done | bytes 270368 | tf_op jit(solution)/shard_map/ppermute | solution.py:34
  36.9 0.8 %unpack.1 = f32[512,256]{1,0:T(8,128)} custom-call(s16[528,256]{1,0:T(8,128)(2,1)S(1)} %collective-permute-done.1.coded), custom_call_target="tpu_custom_call" | custom-call | tf_op jit(solution)/shard_map/unpack/pallas_call | solution.py:405
Async XLA Ops:
  4.4 20.6 %collective-permute-start = (s16[528,256]{1,0:T(8,128)(2,1)S(1)}, s16[528,256]{1,0:T(8,128)(2,1)S(1)}, u32[]{:S(2)}, u32[]{:S(2)}) collective-permute-start(s16[528,256]{1,0:T(8,128)(2,1)S(1)} %get-tuple-element.14), channel_id=1, source_target_pairs={{0,8},{8,16},{16,24},{24,32},{32,40},{40,48},{48,56},{56,64},{64,7... | collective-permute-start | bytes 811016 | tf_op jit(solution)/shard_map/ppermute | solution.py:34
  27.3 9.6 %collective-permute-start.1 = (s16[528,256]{1,0:T(8,128)(2,1)S(1)}, s16[528,256]{1,0:T(8,128)(2,1)S(1)}, u32[]{:S(2)}, u32[]{:S(2)}) collective-permute-start(s16[528,256]{1,0:T(8,128)(2,1)S(1)} %get-tuple-element.17), channel_id=1, source_target_pairs={{0,504},{8,0},{16,8},{24,16},{32,24},{40,32},{48,40},{56,48},{64,5... | collective-permute-start | bytes 811016 | tf_op jit(solution)/shard_map/ppermute | solution.py:34
